TPU v7x, 256 devices: a whole 4x4x8 slice. The times are simulated.
256 devices in a mesh: pool: 32 (over z, y_hi, core), tensor: 8 (over y_lo, x).
Axes of the slice: x: 4, y: 4 (y_hi: 2, y_lo: 2; y = y_hi * 2 + y_lo), z: 8, core: 2. Of those that a mesh axis runs over, the one named last changes fastest.
Arguments:
- queries: bfloat16 [8192, 8192], P(('pool', 'tensor')), may hold values from -4.5 to 4.5
- new_keys: bfloat16 [8192, 1024], P(('pool', 'tensor')), may hold values from -4.5 to 4.5
- new_values: bfloat16 [8192, 1024], P(('pool', 'tensor')), may hold values from -40 to 40
- pool_keys: bfloat16 [8192, 16, 1024], P('pool', None, 'tensor'), may hold values from -4.5 to 4.5
- pool_values: bfloat16 [8192, 16, 1024], P('pool', None, 'tensor'), may hold values from -40 to 40
- prefix_blocks: int32 [32, 256], replicated, may hold values from 0 to 8191, as said below
- block_owner: int32 [8192], replicated, may hold values from 0 to 31, as said below
- block_slot: int32 [8192], replicated, may hold values from 0 to 255
- evict_slots: int32 [32, 16], replicated, may hold values from 0 to 8191, as said below
- tok_counts: int32 [32], replicated, may hold values from 1 to 256, 5120 in all
Outputs:
- attended: bfloat16 [8192, 8192], P(('pool', 'tensor'))
- new_pool_keys: bfloat16 [8192, 16, 1024], P('pool', None, 'tensor')
- new_pool_values: bfloat16 [8192, 16, 1024], P('pool', None, 'tensor')
Inputs may be any that keep to these rules, and one draw needn't show every extreme that they name: `block_owner`: together with block_slot it puts every block in its own slot. `prefix_blocks`: A group's 256 ids are distinct; at most 12 of them are held by one owner, and in each group some owner holds exactly 12. Groups share blocks. `evict_slots`: all entries are distinct; at most 1 of a group's blocks go to one owner (slot // 256), and one owner receives exactly 1 from every group. `tok_counts`: one group has 256 live tokens.
All inputs are finite; a program needn't handle non-finite values.
Results may differ from a plain program's by a relative error of at most 0.0065.
Values may be sent and summed in bfloat16 or wider, within the bound.
No kernel may reach another device: no remote copies, remote signals or barrier semaphores. Data moves between devices by JAX's collectives and lax.ppermute only.
A program may use at most 64 MiB of HBM per device.

v0:
```python
import jax
import jax.numpy as jnp
from jax import lax
from jax.sharding import PartitionSpec as P

H = 64
KVH = 8
HD = 128


neg_big = -1e30


def ranked_pick(selected, values, capacity):
    length = selected.shape[1]
    taken = selected.astype(jnp.bfloat16)
    lower = jnp.arange(length, dtype=jnp.int32)
    triangle = (lower[:, None] <= lower[None, :]).astype(jnp.bfloat16)
    rank = jnp.dot(taken, triangle, preferred_element_type=jnp.float32).astype(jnp.int32) - 1
    chosen = selected.astype(jnp.int32)
    places = jnp.arange(capacity, dtype=jnp.int32)
    hits = chosen[:, :, None] * (rank[:, :, None] == places[None, None, :]).astype(jnp.int32)
    picked = jnp.sum(hits * values[:, :, None], axis=1)
    live = jnp.sum(hits, axis=1) > 0
    return (picked, live)


def select_rows(table, index, live):
    rows, blk, width = table.shape
    lead = index.shape
    flat_index = index.reshape(-1)
    flat_live = live.reshape(-1)
    choose = (
        (flat_index[:, None] == jnp.arange(rows, dtype=jnp.int32)[None, :]) & flat_live[:, None]
    ).astype(table.dtype)
    taken = jnp.dot(choose, table.reshape(rows, blk * width), preferred_element_type=jnp.float32)
    return taken.astype(table.dtype).reshape(lead + (blk, width))


def place_rows(table, destination, incoming):
    rows, blk, width = table.shape
    match = jnp.arange(rows, dtype=jnp.int32)[:, None] == destination[None, :]
    written = jnp.dot(
        match.astype(incoming.dtype),
        incoming.reshape(incoming.shape[0], blk * width),
        preferred_element_type=jnp.float32,
    )
    written = written.astype(table.dtype).reshape(rows, blk, width)
    hit = jnp.any(match, axis=1)
    return jnp.where(hit[:, None, None], written, table)


def absorb(carry, query_heads, keys_block, values_block, mask):
    best, total, summed = carry
    count = keys_block.shape[0]
    kv_local = query_heads.shape[1]
    keys_heads = keys_block.reshape(count, kv_local, HD)
    values_heads = values_block.reshape(count, kv_local, HD)
    scores = jnp.einsum(
        "tkgd,skd->kgts", query_heads, keys_heads, preferred_element_type=jnp.float32
    ) * HD ** (-0.5)
    scores = jnp.where(mask, scores, neg_big)
    fresh = jnp.maximum(best, jnp.max(scores, axis=3))
    shrink = jnp.exp(best - fresh)
    weights = jnp.where(mask, jnp.exp(scores - fresh[..., None]), 0.0)
    total = total * shrink + jnp.sum(weights, axis=3)
    summed = summed * shrink[..., None] + jnp.einsum(
        "kgts,skd->kgtd",
        weights.astype(jnp.bfloat16),
        values_heads,
        preferred_element_type=jnp.float32,
    )
    return (fresh, total, summed)


def attend_prefix(carry, query_heads, got_keys, got_values, got_live):
    sources, capx, blk, width = got_keys.shape
    per = 1
    while per * 2 <= sources and sources % (per * 2) == 0 and (per * 2 * capx * blk <= 1024):
        per = per * 2
    steps = sources // per
    keys_steps = got_keys.reshape(steps, per * capx * blk, width)
    values_steps = got_values.reshape(steps, per * capx * blk, width)
    live_steps = jnp.broadcast_to(got_live[:, :, None], (sources, capx, blk)).reshape(
        steps, per * capx * blk
    )

    def one_step(state, pieces):
        keys_block, values_block, live_block = pieces
        return (
            absorb(state, query_heads, keys_block, values_block, live_block[None, None, None, :]),
            None,
        )

    carry, unused = lax.scan(one_step, carry, (keys_steps, values_steps, live_steps))
    return carry


def local(
    queries,
    new_keys,
    new_values,
    pool_keys,
    pool_values,
    prefix_blocks,
    block_owner,
    block_slot,
    evict_slots,
    tok_counts,
):
    n_pool = lax.axis_size("pool")
    me = lax.axis_index("pool")
    slot_count, blk, width = pool_keys.shape
    head_q, head_k, head_v = (
        lax.all_to_all(queries, "tensor", split_axis=1, concat_axis=0, tiled=True),
        lax.all_to_all(new_keys, "tensor", split_axis=1, concat_axis=0, tiled=True),
        lax.all_to_all(new_values, "tensor", split_axis=1, concat_axis=0, tiled=True),
    )
    tok = head_q.shape[0]
    kv_local = width // HD
    group = H // KVH
    query_heads = head_q.reshape(tok, kv_local, group, HD)
    count = tok_counts[me]
    held = (block_owner * slot_count + block_slot)[prefix_blocks]
    owners = held // slot_count
    slots = held % slot_count
    capacity = 3 * prefix_blocks.shape[1] // (2 * n_pool)
    picked, live = ranked_pick(owners == me, slots, capacity)
    send_keys = select_rows(pool_keys, picked, live)
    send_values = select_rows(pool_values, picked, live)
    my_owners = owners[me]
    sources = jnp.arange(n_pool, dtype=jnp.int32)
    arrivals = jnp.sum((my_owners[None, :] == sources[:, None]).astype(jnp.int32), axis=1)
    got_live = jnp.arange(capacity, dtype=jnp.int32)[None, :] < arrivals[:, None]
    position = jnp.arange(tok, dtype=jnp.int32)
    causal = position[None, :] <= position[:, None]
    state_shape = (kv_local, group, tok)
    carry = (
        jnp.full(state_shape, neg_big, jnp.float32),
        jnp.zeros(state_shape, jnp.float32),
        jnp.zeros(state_shape + (HD,), jnp.float32),
    )
    carry = absorb(carry, query_heads, head_k, head_v, causal)
    got_keys, got_values = (
        lax.all_to_all(send_keys, "pool", split_axis=0, concat_axis=0, tiled=True),
        lax.all_to_all(send_values, "pool", split_axis=0, concat_axis=0, tiled=True),
    )
    carry = attend_prefix(carry, query_heads, got_keys, got_values, got_live)
    best, total, summed = carry
    result = summed / total[..., None]
    result = jnp.transpose(result, (2, 0, 1, 3)).reshape(tok, kv_local * group * HD)
    result = jnp.where((position < count)[:, None], result, 0.0).astype(jnp.bfloat16)
    attended = lax.all_to_all(result, "tensor", split_axis=0, concat_axis=1, tiled=True)
    keep = (position < count)[:, None]
    fresh_keys = jnp.where(keep, head_k, jnp.zeros((), head_k.dtype)).reshape(
        tok // blk, blk, width
    )
    fresh_values = jnp.where(keep, head_v, jnp.zeros((), head_v.dtype)).reshape(
        tok // blk, blk, width
    )
    targets = evict_slots // slot_count
    places = evict_slots % slot_count
    new_blocks = tok // blk
    write_cap = (new_blocks + n_pool - 1) // n_pool
    my_targets = targets[me]
    block_index = jnp.broadcast_to(
        jnp.arange(new_blocks, dtype=jnp.int32)[None, :], (n_pool, new_blocks)
    )
    chosen, sent = ranked_pick(my_targets[None, :] == sources[:, None], block_index, write_cap)
    out_keys = select_rows(fresh_keys, chosen, sent)
    out_values = select_rows(fresh_values, chosen, sent)
    arrived_keys, arrived_values = (
        lax.all_to_all(out_keys, "pool", split_axis=0, concat_axis=0, tiled=True),
        lax.all_to_all(out_values, "pool", split_axis=0, concat_axis=0, tiled=True),
    )
    incoming_keys = arrived_keys.reshape(-1, blk, width)
    incoming_values = arrived_values.reshape(-1, blk, width)
    got_slot, got_ok = ranked_pick(targets == me, places, write_cap)
    destination = jnp.where(got_ok, got_slot, slot_count).reshape(-1)
    new_pool_keys = place_rows(pool_keys, destination, incoming_keys)
    new_pool_values = place_rows(pool_values, destination, incoming_values)
    return (attended, new_pool_keys, new_pool_values)


def solution(mesh):
    placed = (
        P(("pool", "tensor"), None),
        P(("pool", "tensor"), None),
        P(("pool", "tensor"), None),
        P("pool", None, "tensor"),
        P("pool", None, "tensor"),
        P(),
        P(),
        P(),
        P(),
        P(),
    )
    return jax.shard_map(
        local,
        mesh=mesh,
        in_specs=placed,
        out_specs=(
            P(("pool", "tensor"), None),
            P("pool", None, "tensor"),
            P("pool", None, "tensor"),
        ),
        check_vma=False,
    )
```

profile of v0, /device:TPU:1, one launch (start us, length us, event | category | flops | bytes accessed | tf_op | source)
XLA Modules:
  0.0 282.3 jit_solution(10615294640072478138)
XLA Ops:
  2.1 5.9 %all-to-all-start = ((bf16[32,8,128]{2,0,1:T(8,128)(2,1)}), bf16[32,8,128]{2,0,1:T(8,128)(2,1)S(1)}, u32[]{:S(2)}, u32[]{:S(2)}) async-start(bf16[32,8,128]{2,0,1:T(8,128)(2,1)} %copy_bitcast_fusion.2), calls=%async_computation | async-start | bytes 131072 | tf_op jit(solution)/shard_map/all_to_all | solution.py:116
  9.6 45.5 %gather_fusion = s32[8192]{0:T(1024)S(1)} fusion(s32[8192]{0:T(1024)S(1)} %get-tuple-element.116, s32[8192]{0:T(1024)S(1)} %get-tuple-element.117), kind=kCustom, calls=%fused_computation | custom fusion | bytes 98304 | tf_op jit(solution)/shard_map/gather | solution.py:124
  57.4 5.2 %all-to-all-start.2 = ((bf16[32,8,128]{2,0,1:T(8,128)(2,1)}), bf16[32,8,128]{2,0,1:T(8,128)(2,1)S(1)}, u32[]{:S(2)}, u32[]{:S(2)}) async-start(bf16[32,8,128]{2,0,1:T(8,128)(2,1)} %copy_bitcast_fusion.1), calls=%async_computation.2 | async-start | bytes 131072 | tf_op jit(solution)/shard_map/all_to_all | solution.py:117
  63.6 4.1 %all-to-all-done.2 = bf16[32,8,128]{2,0,1:T(8,128)(2,1)S(1)} async-done(((bf16[32,8,128]{2,0,1:T(8,128)(2,1)}), bf16[32,8,128]{2,0,1:T(8,128)(2,1)S(1)}, u32[]{:S(2)}, u32[]{:S(2)}) %all-to-all-start.2) | async-done | bytes 65568 | tf_op jit(solution)/shard_map/all_to_all | solution.py:117
  67.8 13.6 %all-to-all-start.6 = ((bf16[32,1,16,128]{3,2,1,0:T(8,128)(2,1)}), bf16[32,1,16,128]{3,2,1,0:T(8,128)(2,1)S(1)}, u32[]{:S(2)}, u32[]{:S(2)}) async-start(bf16[32,1,16,128]{3,2,1,0:T(8,128)(2,1)} %bitcast.33), calls=%async_computation.6 | async-start | bytes 262144 | tf_op jit(solution)/shard_map/all_to_all | solution.py:173
  82.4 9.7 %all-to-all-done.6 = bf16[32,1,16,128]{3,2,1,0:T(8,128)(2,1)S(1)} async-done(((bf16[32,1,16,128]{3,2,1,0:T(8,128)(2,1)}), bf16[32,1,16,128]{3,2,1,0:T(8,128)(2,1)S(1)}, u32[]{:S(2)}, u32[]{:S(2)}) %all-to-all-start.6) | async-done | bytes 131104 | tf_op jit(solution)/shard_map/all_to_all | solution.py:173
  92.2 3.5 %all-to-all-start.1 = ((bf16[32,8,1024]{2,0,1:T(8,128)(2,1)}), bf16[32,8,1024]{2,0,1:T(8,128)(2,1)S(1)}, u32[]{:S(2)}, u32[]{:S(2)}) async-start(bf16[32,8,1024]{2,0,1:T(8,128)(2,1)} %bitcast.200), calls=%async_computation.1 | async-start | bytes 1048576 | tf_op jit(solution)/shard_map/all_to_all | solution.py:115
  98.8 7.1 %all-to-all-done.1 = bf16[32,8,1024]{2,0,1:T(8,128)(2,1)S(1)} async-done(((bf16[32,8,1024]{2,0,1:T(8,128)(2,1)}), bf16[32,8,1024]{2,0,1:T(8,128)(2,1)S(1)}, u32[]{:S(2)}, u32[]{:S(2)}) %all-to-all-start.1) | async-done | bytes 524320 | tf_op jit(solution)/shard_map/all_to_all | solution.py:115
  105.9 5.0 %all-to-all-start.3 = ((bf16[32,12,16,128]{3,2,1,0:T(8,128)(2,1)}), bf16[32,12,16,128]{3,2,1,0:T(8,128)(2,1)}, u32[]{:S(2)}, u32[]{:S(2)}) async-start(bf16[32,12,16,128]{3,2,1,0:T(8,128)(2,1)} %bitcast.57), calls=%async_computation.3 | async-start | bytes 3145728 | tf_op jit(solution)/shard_map/all_to_all | solution.py:145
  113.2 37.0 %all-to-all-done.3 = bf16[32,12,16,128]{3,2,1,0:T(8,128)(2,1)} async-done(((bf16[32,12,16,128]{3,2,1,0:T(8,128)(2,1)}), bf16[32,12,16,128]{3,2,1,0:T(8,128)(2,1)}, u32[]{:S(2)}, u32[]{:S(2)}) %all-to-all-start.3) | async-done | bytes 1572896 | tf_op jit(solution)/shard_map/all_to_all | solution.py:145
  150.2 6.1 %all-to-all-start.4 = ((bf16[32,12,16,128]{3,2,1,0:T(8,128)(2,1)}), bf16[32,12,16,128]{3,2,1,0:T(8,128)(2,1)}, u32[]{:S(2)}, u32[]{:S(2)}) async-start(bf16[32,12,16,128]{3,2,1,0:T(8,128)(2,1)} %bitcast.67), calls=%async_computation.4 | async-start | bytes 3145728 | tf_op jit(solution)/shard_map/all_to_all | solution.py:146
  163.5 32.1 %all-to-all-done.4 = bf16[32,12,16,128]{3,2,1,0:T(8,128)(2,1)} async-done(((bf16[32,12,16,128]{3,2,1,0:T(8,128)(2,1)}), bf16[32,12,16,128]{3,2,1,0:T(8,128)(2,1)}, u32[]{:S(2)}, u32[]{:S(2)}) %all-to-all-start.4) | async-done | bytes 1572896 | tf_op jit(solution)/shard_map/all_to_all | solution.py:146
  195.6 6.0 %all-to-all-start.7 = ((bf16[32,1,16,128]{3,2,1,0:T(8,128)(2,1)}), bf16[32,1,16,128]{3,2,1,0:T(8,128)(2,1)S(1)}, u32[]{:S(2)}, u32[]{:S(2)}) async-start(bf16[32,1,16,128]{3,2,1,0:T(8,128)(2,1)} %bitcast.34), calls=%async_computation.7 | async-start | bytes 262144 | tf_op jit(solution)/shard_map/all_to_all | solution.py:174
  201.6 61.2 %while.14 = (s32[]{:T(128)}, f32[1,8,256]{2,1,0:T(8,128)S(1)}, f32[1,8,256]{2,1,0:T(8,128)S(1)}, f32[1,8,256,128]{3,2,1,0:T(8,128)}, pred[8,768]{1,0:T(8,128)(4,...) while((s32[]{:T(128)}, f32[1,8,256]{2,1,0:T(8,128)S(1)}, ...), condition=%wide.region_8.9_spmd, body=%wide.region_5.8_spmd.sunk | while | flops 826284032 | bytes 30415000 | solution.py:95
  203.7 3.4 %fusion.114 = f32[1,8,256,128]{3,2,1,0:T(8,128)S(1)} fusion(f32[768,256,8]{1,0,2:T(8,128)S(1)} %get-tuple-element.173, f32[8,256]{1,0:T(8,128)S(1)} %bitcast.233, pred[768]{0:T(1024)(128)(4,1)S(1)} %dynamic-slice_reduce_fusion.3, f32[1,8,256,128]{3,2,1,0:T(8,128)S(1)} %copy-done.4, f32[8,256]{1,0:T(8,128)S(1)} %get-tuple-element.174, ...), kind=kOutput, calls=%fused_computation.13.clone.1 | convolution fusion | flops 411041792 | bytes 8604160 | tf_op jit(solution)/shard_map/while/body/eval_jaxpr/kgts,skd->kgtd/dot_general | solution.py:67
  211.4 3.4 %fusion.114 = f32[1,8,256,128]{3,2,1,0:T(8,128)S(1)} fusion(f32[768,256,8]{1,0,2:T(8,128)S(1)} %get-tuple-element.173, f32[8,256]{1,0:T(8,128)S(1)} %bitcast.233, pred[768]{0:T(1024)(128)(4,1)S(1)} %dynamic-slice_reduce_fusion.3, f32[1,8,256,128]{3,2,1,0:T(8,128)S(1)} %copy-done.4, f32[8,256]{1,0:T(8,128)S(1)} %get-tuple-element.174, ...), kind=kOutput, calls=%fused_computation.13.clone.1 | convolution fusion | flops 411041792 | bytes 8604160 | tf_op jit(solution)/shard_map/while/body/eval_jaxpr/kgts,skd->kgtd/dot_general | solution.py:67
  219.0 3.4 %fusion.114 = f32[1,8,256,128]{3,2,1,0:T(8,128)S(1)} fusion(f32[768,256,8]{1,0,2:T(8,128)S(1)} %get-tuple-element.173, f32[8,256]{1,0:T(8,128)S(1)} %bitcast.233, pred[768]{0:T(1024)(128)(4,1)S(1)} %dynamic-slice_reduce_fusion.3, f32[1,8,256,128]{3,2,1,0:T(8,128)S(1)} %copy-done.4, f32[8,256]{1,0:T(8,128)S(1)} %get-tuple-element.174, ...), kind=kOutput, calls=%fused_computation.13.clone.1 | convolution fusion | flops 411041792 | bytes 8604160 | tf_op jit(solution)/shard_map/while/body/eval_jaxpr/kgts,skd->kgtd/dot_general | solution.py:67
  226.7 3.4 %fusion.114 = f32[1,8,256,128]{3,2,1,0:T(8,128)S(1)} fusion(f32[768,256,8]{1,0,2:T(8,128)S(1)} %get-tuple-element.173, f32[8,256]{1,0:T(8,128)S(1)} %bitcast.233, pred[768]{0:T(1024)(128)(4,1)S(1)} %dynamic-slice_reduce_fusion.3, f32[1,8,256,128]{3,2,1,0:T(8,128)S(1)} %copy-done.4, f32[8,256]{1,0:T(8,128)S(1)} %get-tuple-element.174, ...), kind=kOutput, calls=%fused_computation.13.clone.1 | convolution fusion | flops 411041792 | bytes 8604160 | tf_op jit(solution)/shard_map/while/body/eval_jaxpr/kgts,skd->kgtd/dot_general | solution.py:67
  234.3 3.4 %fusion.114 = f32[1,8,256,128]{3,2,1,0:T(8,128)S(1)} fusion(f32[768,256,8]{1,0,2:T(8,128)S(1)} %get-tuple-element.173, f32[8,256]{1,0:T(8,128)S(1)} %bitcast.233, pred[768]{0:T(1024)(128)(4,1)S(1)} %dynamic-slice_reduce_fusion.3, f32[1,8,256,128]{3,2,1,0:T(8,128)S(1)} %copy-done.4, f32[8,256]{1,0:T(8,128)S(1)} %get-tuple-element.174, ...), kind=kOutput, calls=%fused_computation.13.clone.1 | convolution fusion | flops 411041792 | bytes 8604160 | tf_op jit(solution)/shard_map/while/body/eval_jaxpr/kgts,skd->kgtd/dot_general | solution.py:67
  242.0 3.4 %fusion.114 = f32[1,8,256,128]{3,2,1,0:T(8,128)S(1)} fusion(f32[768,256,8]{1,0,2:T(8,128)S(1)} %get-tuple-element.173, f32[8,256]{1,0:T(8,128)S(1)} %bitcast.233, pred[768]{0:T(1024)(128)(4,1)S(1)} %dynamic-slice_reduce_fusion.3, f32[1,8,256,128]{3,2,1,0:T(8,128)S(1)} %copy-done.4, f32[8,256]{1,0:T(8,128)S(1)} %get-tuple-element.174, ...), kind=kOutput, calls=%fused_computation.13.clone.1 | convolution fusion | flops 411041792 | bytes 8604160 | tf_op jit(solution)/shard_map/while/body/eval_jaxpr/kgts,skd->kgtd/dot_general | solution.py:67
  249.6 3.4 %fusion.114 = f32[1,8,256,128]{3,2,1,0:T(8,128)S(1)} fusion(f32[768,256,8]{1,0,2:T(8,128)S(1)} %get-tuple-element.173, f32[8,256]{1,0:T(8,128)S(1)} %bitcast.233, pred[768]{0:T(1024)(128)(4,1)S(1)} %dynamic-slice_reduce_fusion.3, f32[1,8,256,128]{3,2,1,0:T(8,128)S(1)} %copy-done.4, f32[8,256]{1,0:T(8,128)S(1)} %get-tuple-element.174, ...), kind=kOutput, calls=%fused_computation.13.clone.1 | convolution fusion | flops 411041792 | bytes 8604160 | tf_op jit(solution)/shard_map/while/body/eval_jaxpr/kgts,skd->kgtd/dot_general | solution.py:67
  257.2 3.4 %fusion.114 = f32[1,8,256,128]{3,2,1,0:T(8,128)S(1)} fusion(f32[768,256,8]{1,0,2:T(8,128)S(1)} %get-tuple-element.173, f32[8,256]{1,0:T(8,128)S(1)} %bitcast.233, pred[768]{0:T(1024)(128)(4,1)S(1)} %dynamic-slice_reduce_fusion.3, f32[1,8,256,128]{3,2,1,0:T(8,128)S(1)} %copy-done.4, f32[8,256]{1,0:T(8,128)S(1)} %get-tuple-element.174, ...), kind=kOutput, calls=%fused_computation.13.clone.1 | convolution fusion | flops 411041792 | bytes 8604160 | tf_op jit(solution)/shard_map/while/body/eval_jaxpr/kgts,skd->kgtd/dot_general | solution.py:67
  265.9 4.3 %all-to-all-start.5 = ((bf16[8,32,1024]{2,1,0:T(8,128)(2,1)}), bf16[8,32,1024]{2,1,0:T(8,128)(2,1)}, u32[]{:S(2)}, u32[]{:S(2)}) async-start(bf16[8,32,1024]{2,1,0:T(8,128)(2,1)} %select_convert_fusion), calls=%async_computation.5 | async-start | bytes 1048576 | tf_op jit(solution)/shard_map/all_to_all | solution.py:153
  273.0 7.5 %all-to-all-done.5 = bf16[8,32,1024]{2,1,0:T(8,128)(2,1)} async-done(((bf16[8,32,1024]{2,1,0:T(8,128)(2,1)}), bf16[8,32,1024]{2,1,0:T(8,128)(2,1)}, u32[]{:S(2)}, u32[]{:S(2)}) %all-to-all-start.5) | async-done | bytes 524320 | tf_op jit(solution)/shard_map/all_to_all | solution.py:153
  (158 shorter events, 60.5 us)
Async XLA Ops:
  2.1 55.3 %all-to-all-start = ((bf16[32,8,128]{2,0,1:T(8,128)(2,1)}), bf16[32,8,128]{2,0,1:T(8,128)(2,1)S(1)}, u32[]{:S(2)}, u32[]{:S(2)}) async-start(bf16[32,8,128]{2,0,1:T(8,128)(2,1)} %copy_bitcast_fusion.2), calls=%async_computation | async-start | bytes 131072 | tf_op jit(solution)/shard_map/all_to_all | solution.py:116
  9.6 45.6 %copy-start.7 = (bf16[32,1024]{1,0:T(8,128)(2,1)S(1)}, bf16[32,1024]{1,0:T(8,128)(2,1)}, u32[]{:S(2)}) copy-start(bf16[32,1024]{1,0:T(8,128)(2,1)} %param.14) | copy-start | bytes 196612
  9.6 46.3 %copy-start.8 = (s32[32,16]{0,1:T(8,128)S(1)}, s32[32,16]{0,1:T(8,128)}, u32[]{:S(2)}) copy-start(s32[32,16]{0,1:T(8,128)} %param.20) | copy-start | bytes 6148
  9.6 46.3 %copy-start.9 = (s32[32]{0:T(128)S(1)}, s32[32]{0:T(128)}, u32[]{:S(2)}) copy-start(s32[32]{0:T(128)} %param.21) | copy-start | bytes 388
  9.6 72.0 %copy-start.6 = (bf16[32,8192]{1,0:T(8,128)(2,1)S(1)}, bf16[32,8192]{1,0:T(8,128)(2,1)}, u32[]{:S(2)}) copy-start(bf16[32,8192]{1,0:T(8,128)(2,1)} %param.12) | copy-start | bytes 1572868
  55.1 41.5 %copy-start.1 = (bf16[256,16,128]{2,1,0:T(8,128)(2,1)S(1)}, bf16[256,16,128]{2,1,0:T(8,128)(2,1)}, u32[]{:S(2)}) copy-start(bf16[256,16,128]{2,1,0:T(8,128)(2,1)} %param.15) | copy-start | bytes 3145732
  57.4 10.4 %all-to-all-start.2 = ((bf16[32,8,128]{2,0,1:T(8,128)(2,1)}), bf16[32,8,128]{2,0,1:T(8,128)(2,1)S(1)}, u32[]{:S(2)}, u32[]{:S(2)}) async-start(bf16[32,8,128]{2,0,1:T(8,128)(2,1)} %copy_bitcast_fusion.1), calls=%async_computation.2 | async-start | bytes 131072 | tf_op jit(solution)/shard_map/all_to_all | solution.py:117
  67.8 24.4 %all-to-all-start.6 = ((bf16[32,1,16,128]{3,2,1,0:T(8,128)(2,1)}), bf16[32,1,16,128]{3,2,1,0:T(8,128)(2,1)S(1)}, u32[]{:S(2)}, u32[]{:S(2)}) async-start(bf16[32,1,16,128]{3,2,1,0:T(8,128)(2,1)} %bitcast.33), calls=%async_computation.6 | async-start | bytes 262144 | tf_op jit(solution)/shard_map/all_to_all | solution.py:173
  92.2 13.7 %all-to-all-start.1 = ((bf16[32,8,1024]{2,0,1:T(8,128)(2,1)}), bf16[32,8,1024]{2,0,1:T(8,128)(2,1)S(1)}, u32[]{:S(2)}, u32[]{:S(2)}) async-start(bf16[32,8,1024]{2,0,1:T(8,128)(2,1)} %bitcast.200), calls=%async_computation.1 | async-start | bytes 1048576 | tf_op jit(solution)/shard_map/all_to_all | solution.py:115
  98.8 12.2 %copy-start.2 = (bf16[256,16,128]{2,1,0:T(8,128)(2,1)S(1)}, bf16[256,16,128]{2,1,0:T(8,128)(2,1)}, u32[]{:S(2)}) copy-start(bf16[256,16,128]{2,1,0:T(8,128)(2,1)} %param.16) | copy-start | bytes 3145732
  105.9 44.3 %all-to-all-start.3 = ((bf16[32,12,16,128]{3,2,1,0:T(8,128)(2,1)}), bf16[32,12,16,128]{3,2,1,0:T(8,128)(2,1)}, u32[]{:S(2)}, u32[]{:S(2)}) async-start(bf16[32,12,16,128]{3,2,1,0:T(8,128)(2,1)} %bitcast.57), calls=%async_computation.3 | async-start | bytes 3145728 | tf_op jit(solution)/shard_map/all_to_all | solution.py:145
  150.2 45.4 %all-to-all-start.4 = ((bf16[32,12,16,128]{3,2,1,0:T(8,128)(2,1)}), bf16[32,12,16,128]{3,2,1,0:T(8,128)(2,1)}, u32[]{:S(2)}, u32[]{:S(2)}) async-start(bf16[32,12,16,128]{3,2,1,0:T(8,128)(2,1)} %bitcast.67), calls=%async_computation.4 | async-start | bytes 3145728 | tf_op jit(solution)/shard_map/all_to_all | solution.py:146
  195.6 70.3 %all-to-all-start.7 = ((bf16[32,1,16,128]{3,2,1,0:T(8,128)(2,1)}), bf16[32,1,16,128]{3,2,1,0:T(8,128)(2,1)S(1)}, u32[]{:S(2)}, u32[]{:S(2)}) async-start(bf16[32,1,16,128]{3,2,1,0:T(8,128)(2,1)} %bitcast.34), calls=%async_computation.7 | async-start | bytes 262144 | tf_op jit(solution)/shard_map/all_to_all | solution.py:174
  201.6 2.1 copy-start.4
  207.2 2.0 copy-start.5
  209.3 2.1 copy-start.4
  216.9 2.1 copy-start.4
  224.6 2.1 copy-start.4
  232.2 2.1 copy-start.4
  239.9 2.1 copy-start.4
  247.5 2.1 copy-start.4
  255.2 2.1 copy-start.4
  265.9 5.1 %copy-start.3 = (bf16[32,8,16,128]{3,2,1,0:T(8,128)(2,1)S(1)}, bf16[32,8,16,128]{3,2,1,0:T(8,128)(2,1)}, u32[]{:S(2)}) copy-start(bf16[32,8,16,128]{3,2,1,0:T(8,128)(2,1)} %copy.74) | copy-start | bytes 3145732
  265.9 14.6 %all-to-all-start.5 = ((bf16[8,32,1024]{2,1,0:T(8,128)(2,1)}), bf16[8,32,1024]{2,1,0:T(8,128)(2,1)}, u32[]{:S(2)}, u32[]{:S(2)}) async-start(bf16[8,32,1024]{2,1,0:T(8,128)(2,1)} %select_convert_fusion), calls=%async_computation.5 | async-start | bytes 1048576 | tf_op jit(solution)/shard_map/all_to_all | solution.py:153
  (8 other events, 15.1 us)
where the time goes:
time: 284 us; the launch traced here: 282 us
  waiting for transfers between devices  97.6 us (34%)
  local copies, waits for them, and re-layouts  59 us (21%)
  starting transfers between devices  49.6 us (17%)
  matrix products  49.5 us (17%)
  other arithmetic  24.9 us (9%)
    gather x2, local copies, waits for them, and re-layouts, local(): held = (block_owner * slot_count + block_slot)[prefix_blocks]  45.5 us
    all_to_all x1, waiting for transfers between devices, local(): lax.all_to_all(send_keys, 'pool', split_axis=0, concat_axis=0, tiled=True)  37 us
    all_to_all x1, waiting for transfers between devices, local(): lax.all_to_all(send_values, 'pool', split_axis=0, concat_axis=0, tiled=True)  32.1 us
    dot_general x9, matrix products, absorb(): jnp.einsum('kgts,skd->kgtd', weights.astype(jnp.bfloat16), values_heads,...  29.3 us
    dot_general x9, matrix products, absorb(): jnp.einsum('tkgd,skd->kgts', query_heads, keys_heads, preferred_element_t...  16.9 us
    reduce_sum x9, other arithmetic, absorb(): total = total * shrink + jnp.sum(weights, axis=3)  16.7 us
    all_to_all x1, starting transfers between devices, local(): lax.all_to_all(out_keys, 'pool', split_axis=0, concat_axis=0, tiled=True)  13.6 us
    all_to_all x1, waiting for transfers between devices, local(): lax.all_to_all(out_keys, 'pool', split_axis=0, concat_axis=0, tiled=True)  9.75 us
  transfers between devices with their start and end apart: 8, of which 6 were waited for; matrix products, arithmetic and copies ran while one was open for 46% of the time, Pallas kernels for 0%

commit v1 on v0

v1 whole, which is shorter than its diff:
```python
import jax
import jax.numpy as jnp
from jax import lax
from jax.experimental import pallas as pl
from jax.experimental.pallas import tpu as pltpu
from jax.sharding import PartitionSpec as P

H = 64
KVH = 8
HD = 128
GROUP = H // KVH
BLK = 16
POOL = 32
PLANE = 4
LEVELS = 8
TENSOR = 8
SLOTS = 256
PBLK = 256
CAP = 12
TOK = 256
PIECE = (GROUP + 2) * HD
STEP = 4
SCALE = HD ** (-0.5) * 1.4426950408889634
neg_big = -1e30

bf16 = jnp.bfloat16
f32 = jnp.float32
i32 = jnp.int32

VMEM = pl.BlockSpec(memory_space=pltpu.VMEM)
SMEM = pl.BlockSpec(memory_space=pltpu.SMEM)


def cost(flops, moved, exps=0):
    return pl.CostEstimate(flops=flops, bytes_accessed=moved, transcendentals=exps)


def pack_kernel(me, prefix, owner, slot, keys, values, out, wanted, picked, picked_s, sem):
    step = pl.program_id(0)

    @pl.when(step == 0)
    def _():
        rows, lanes = owner.shape
        mine = jnp.where(owner[...] == me[0], slot[...] + 1, 0).astype(f32).astype(bf16)
        lane_of = lax.broadcasted_iota(i32, (lanes, PBLK), 0)
        row_of = lax.broadcasted_iota(i32, (rows, PBLK), 0)
        for g in range(POOL):
            index = prefix[g : g + 1, :]
            low = index & (lanes - 1)
            high = index >> 7
            hot = jnp.where(lane_of == low, 1.0, 0.0).astype(bf16)
            found = jnp.dot(mine, hot, preferred_element_type=f32)
            wanted[g : g + 1, :] = jnp.sum(
                jnp.where(row_of == high, found, 0.0), axis=0, keepdims=True
            )
        place = wanted[...]
        held = place > 0.5
        before = lax.broadcasted_iota(i32, (PBLK, PBLK), 0)
        after = lax.broadcasted_iota(i32, (PBLK, PBLK), 1)
        triangle = jnp.where(before <= after, 1.0, 0.0).astype(bf16)
        rank = jnp.dot(
            jnp.where(held, 1.0, 0.0).astype(bf16), triangle, preferred_element_type=f32
        )
        rank = jnp.where(held, rank, 0.0)
        lane = lax.broadcasted_iota(i32, (POOL, 128), 1)
        chosen = jnp.zeros((POOL, 128), f32)
        for r in range(CAP):
            one = jnp.sum(jnp.where(rank == r + 1.0, place - 1.0, 0.0), axis=1, keepdims=True)
            chosen = jnp.where(lane == r, one, chosen)
        picked[...] = chosen.astype(i32)
        copy = pltpu.make_async_copy(picked, picked_s, sem)
        copy.start()
        copy.wait()

    for g in range(POOL // STEP):
        for r in range(CAP):
            s = picked_s[step * (POOL // STEP) + g, r]
            out[g, r] = keys[s]
            out[g, CAP + r] = values[s]


def pack(me, prefix_blocks, block_owner, block_slot, pool_keys, pool_values):
    whole = lambda shape: pl.BlockSpec(shape, lambda i: (0,) * len(shape))
    table = (block_owner.shape[0] // 128, 128)
    return pl.pallas_call(
        pack_kernel,
        grid=(STEP,),
        out_shape=jax.ShapeDtypeStruct((POOL, 2 * CAP, BLK, HD), bf16),
        in_specs=[
            SMEM,
            whole(prefix_blocks.shape),
            whole(table),
            whole(table),
            whole(pool_keys.shape),
            whole(pool_values.shape),
        ],
        out_specs=pl.BlockSpec((POOL // STEP, 2 * CAP, BLK, HD), lambda i: (i, 0, 0, 0)),
        scratch_shapes=[
            pltpu.VMEM((POOL, PBLK), f32),
            pltpu.VMEM((POOL, 128), i32),
            pltpu.SMEM((POOL, 128), i32),
            pltpu.SemaphoreType.DMA,
        ],
        compiler_params=pltpu.CompilerParams(vmem_limit_bytes=24 * 1024 * 1024),
        cost_estimate=cost(10**9, 5 * 10**6),
        name="pack_blocks",
    )(
        me.reshape(1),
        prefix_blocks,
        block_owner.reshape(table),
        block_slot.reshape(table),
        pool_keys,
        pool_values,
    )


def gather_kernel(info, source, *refs):
    pieces = refs[:TENSOR]
    heads, own_keys, own_values = refs[TENSOR : TENSOR + 3]
    sends = refs[TENSOR + 3 : TENSOR + 3 + LEVELS]
    fresh = refs[-1]
    t, count, level = info[0], info[1], info[2]
    rows = TOK // TENSOR
    for k in range(TENSOR):
        start = pl.multiple_of((t ^ k) * rows, rows)
        at = pl.ds(start, rows)
        for h in range(GROUP):
            heads[h, at, :] = pieces[k][:, h * HD : (h + 1) * HD]
        key_rows = pieces[k][:, GROUP * HD : (GROUP + 1) * HD]
        value_rows = pieces[k][:, (GROUP + 1) * HD :]
        own_keys[at, :] = key_rows
        own_values[at, :] = value_rows
        live = start + lax.broadcasted_iota(i32, (rows, HD), 0) < count
        kept_keys = jnp.where(live, key_rows.astype(f32), 0.0).astype(bf16)
        kept_values = jnp.where(live, value_rows.astype(f32), 0.0).astype(bf16)
        for b in range(rows // BLK):
            block = (t ^ k) * (rows // BLK) + b
            fresh[block, 0] = kept_keys[b * BLK : (b + 1) * BLK]
            fresh[block, 1] = kept_values[b * BLK : (b + 1) * BLK]
    for k in range(LEVELS):
        plane = lax.rem(level + k, LEVELS)
        for r in range(PLANE):
            sends[k][r] = fresh[source[plane * PLANE + r]]


def gather(info, source, pieces):
    return pl.pallas_call(
        gather_kernel,
        out_shape=[
            jax.ShapeDtypeStruct((GROUP, TOK, HD), bf16),
            jax.ShapeDtypeStruct((TOK, HD), bf16),
            jax.ShapeDtypeStruct((TOK, HD), bf16),
        ]
        + [jax.ShapeDtypeStruct((PLANE, 2, BLK, HD), bf16)] * LEVELS,
        in_specs=[SMEM, SMEM] + [VMEM] * TENSOR,
        out_specs=[VMEM] * (3 + LEVELS),
        scratch_shapes=[pltpu.VMEM((TOK // BLK, 2, BLK, HD), bf16)],
        compiler_params=pltpu.CompilerParams(vmem_limit_bytes=16 * 1024 * 1024),
        cost_estimate=cost(10**6, 2 * 10**6),
        name="gather_rows",
    )(info, source, *pieces)


def turn_kernel(info, *refs):
    got = refs[:LEVELS]
    outs = refs[LEVELS:]
    lane = info[3]
    for m in range(PLANE):
        for k in range(LEVELS):
            outs[m][k] = got[k][lane ^ m]


def turn(info, got):
    return pl.pallas_call(
        turn_kernel,
        out_shape=[jax.ShapeDtypeStruct((LEVELS, 2, BLK, HD), bf16)] * PLANE,
        in_specs=[SMEM] + [VMEM] * LEVELS,
        out_specs=[VMEM] * PLANE,
        cost_estimate=cost(10**6, 10**6),
        name="turn_blocks",
    )(info, *got)


def write_kernel(info, target, keys, values, *refs):
    arrived = refs[:PLANE]
    out_keys, out_values = refs[PLANE:]
    level, lane = info[2], info[3]
    out_keys[...] = keys[...]
    out_values[...] = values[...]
    for m in range(PLANE):
        for k in range(LEVELS):
            group = lax.rem(level + LEVELS - k, LEVELS) * PLANE + (lane ^ m)
            slot = target[group]

            @pl.when(slot >= 0)
            def _():
                out_keys[slot] = arrived[m][k, 0]
                out_values[slot] = arrived[m][k, 1]


def write(info, target, pool_keys, pool_values, arrived):
    return pl.pallas_call(
        write_kernel,
        out_shape=[jax.ShapeDtypeStruct(pool_keys.shape, bf16)] * 2,
        in_specs=[SMEM, SMEM] + [VMEM] * (2 + PLANE),
        out_specs=[VMEM] * 2,
        compiler_params=pltpu.CompilerParams(vmem_limit_bytes=16 * 1024 * 1024),
        cost_estimate=cost(10**6, 4 * 10**6),
        name="write_blocks",
    )(info, target, pool_keys, pool_values, *arrived)


KEYS = PBLK * BLK
TILE = 512
TILES = KEYS // TILE
ALL = KEYS + TOK


def attend_kernel(
    info, where_from, heads, next_heads, own_keys, own_values, got, out, keys, values, scores, peak
):
    step = pl.program_id(0)
    slot = lax.rem(step, 2)
    nt = (((1,), (1,)), ((), ()))

    def first_pass(query, into):
        best = None
        for j in range(TILES):
            part = lax.dot_general(
                query, keys[j * TILE : (j + 1) * TILE, :], nt, preferred_element_type=f32
            )
            scores[into, :, j * TILE : (j + 1) * TILE] = part
            for c in range(TILE // 128):
                piece = part[:, c * 128 : (c + 1) * 128]
                best = piece if best is None else jnp.maximum(best, piece)
        part = lax.dot_general(query, own_keys[...], nt, preferred_element_type=f32)
        row = lax.broadcasted_iota(i32, (TOK, TOK), 0)
        column = lax.broadcasted_iota(i32, (TOK, TOK), 1)
        part = jnp.where(column <= row, part, neg_big)
        scores[into, :, KEYS:] = part
        for c in range(TOK // 128):
            best = jnp.maximum(best, part[:, c * 128 : (c + 1) * 128])
        top = jnp.max(best, axis=1, keepdims=True)
        peak[into] = jnp.broadcast_to(top * SCALE, (TOK, 128))

    @pl.when(step == 0)
    def _():
        for b in range(PBLK):
            index = where_from[b]
            keys[b * BLK : (b + 1) * BLK, :] = got[index]
            values[b * BLK : (b + 1) * BLK, :HD] = got[index + CAP]
        values[KEYS:, :HD] = own_values[...]
        values[:, HD:] = jnp.ones((ALL, HD), bf16)
        first_pass(heads[0], 0)

    first_pass(next_heads[0], 1 - slot)
    top = peak[slot]
    summed = jnp.zeros((TOK, 2 * HD), f32)
    for begin, width in [(j * TILE, TILE) for j in range(TILES)] + [(KEYS, TOK)]:
        part = scores[slot, :, begin : begin + width]
        weights = jnp.concatenate(
            [
                jnp.exp2(part[:, c * 128 : (c + 1) * 128] * SCALE - top)
                for c in range(width // 128)
            ],
            axis=1,
        ).astype(bf16)
        summed += jnp.dot(weights, values[begin : begin + width, :], preferred_element_type=f32)
    live = lax.broadcasted_iota(i32, (TOK, HD), 0) < info[1]
    result = summed[:, :HD] / summed[:, HD:]
    out[...] = jnp.where(live, result, 0.0).astype(bf16)


def attend(info, where_from, heads, own_keys, own_values, got):
    whole = lambda shape: pl.BlockSpec(shape, lambda i: (0,) * len(shape))
    blocks = got.shape[0] * got.shape[1]
    return pl.pallas_call(
        attend_kernel,
        grid=(GROUP,),
        out_shape=jax.ShapeDtypeStruct((TOK, GROUP * HD), bf16),
        in_specs=[
            SMEM,
            SMEM,
            pl.BlockSpec((1, TOK, HD), lambda i: (i, 0, 0)),
            pl.BlockSpec((1, TOK, HD), lambda i: (jnp.minimum(i + 1, GROUP - 1), 0, 0)),
            whole((TOK, HD)),
            whole((TOK, HD)),
            whole((blocks, BLK, HD)),
        ],
        out_specs=pl.BlockSpec((TOK, HD), lambda i: (0, i)),
        scratch_shapes=[
            pltpu.VMEM((KEYS, HD), bf16),
            pltpu.VMEM((ALL, 2 * HD), bf16),
            pltpu.VMEM((2, TOK, ALL), f32),
            pltpu.VMEM((2, TOK, 128), f32),
        ],
        compiler_params=pltpu.CompilerParams(vmem_limit_bytes=48 * 1024 * 1024),
        cost_estimate=cost(9 * 10**9, 6 * 10**6, 9 * 10**6),
        name="attend",
    )(info, where_from, heads, heads, own_keys, own_values, got.reshape(blocks, BLK, HD))


def local(
    queries,
    new_keys,
    new_values,
    pool_keys,
    pool_values,
    prefix_blocks,
    block_owner,
    block_slot,
    evict_slots,
    tok_counts,
):
    me = lax.axis_index("pool").astype(i32)
    t = lax.axis_index("tensor").astype(i32)

    send = pack(me, prefix_blocks, block_owner, block_slot, pool_keys, pool_values)
    send, queries, new_keys, new_values = lax.optimization_barrier(
        (send, queries, new_keys, new_values)
    )
    got = lax.all_to_all(send, "pool", split_axis=0, concat_axis=0, tiled=True)

    pieces = []
    for k in range(TENSOR):
        head = t ^ k
        piece = jnp.concatenate(
            [
                lax.dynamic_slice_in_dim(queries, head * GROUP * HD, GROUP * HD, 1),
                lax.dynamic_slice_in_dim(new_keys, head * HD, HD, 1),
                lax.dynamic_slice_in_dim(new_values, head * HD, HD, 1),
            ],
            axis=1,
        )
        if k:
            piece = lax.ppermute(piece, "tensor", [(s, s ^ k) for s in range(TENSOR)])
        pieces.append(piece)

    sources = jnp.arange(POOL, dtype=i32)
    my_owners = block_owner[prefix_blocks[me]]
    ends = jnp.sum((my_owners[None, :] <= sources[:, None]).astype(i32), axis=1)
    starts = jnp.sum((my_owners[None, :] < sources[:, None]).astype(i32), axis=1)
    nth = jnp.arange(PBLK, dtype=i32)
    which = jnp.sum((ends[None, :] <= nth[:, None]).astype(i32), axis=1)
    base = jnp.max(jnp.where(starts[None, :] <= nth[:, None], starts[None, :], 0), axis=1)
    where_from = which * (2 * CAP) + nth - base

    targets = evict_slots // SLOTS
    places = evict_slots % SLOTS
    order = jnp.arange(evict_slots.shape[1], dtype=i32)
    source = jnp.sum(
        jnp.where(targets[me][None, :] == sources[:, None], order[None, :], 0), axis=1
    )
    target = jnp.max(jnp.where(targets == me, places, -1), axis=1)

    info = jnp.stack([t, tok_counts[me], me // PLANE, me % PLANE])
    heads, own_keys, own_values, *sends = gather(info, source, pieces)
    arrived = [sends[0]] + [
        lax.ppermute(
            sends[k], "pool", [(s, (s + PLANE * k) % POOL) for s in range(POOL)]
        )
        for k in range(1, LEVELS)
    ]
    turned = turn(info, arrived)
    arrived = [turned[0]] + [
        lax.ppermute(turned[m], "pool", [(s, s ^ m) for s in range(POOL)])
        for m in range(1, PLANE)
    ]
    new_pool_keys, new_pool_values = write(info, target, pool_keys, pool_values, arrived)

    result = attend(info, where_from, heads, own_keys, own_values, got)
    result = result.reshape(TENSOR, TOK // TENSOR, GROUP * HD)
    attended = lax.all_to_all(result, "tensor", split_axis=0, concat_axis=0, tiled=True)
    attended = jnp.transpose(attended, (1, 0, 2)).reshape(TOK // TENSOR, H * HD)
    return (attended, new_pool_keys, new_pool_values)


def solution(mesh):
    placed = (
        P(("pool", "tensor"), None),
        P(("pool", "tensor"), None),
        P(("pool", "tensor"), None),
        P("pool", None, "tensor"),
        P("pool", None, "tensor"),
        P(),
        P(),
        P(),
        P(),
        P(),
    )
    return jax.shard_map(
        local,
        mesh=mesh,
        in_specs=placed,
        out_specs=(
            P(("pool", "tensor"), None),
            P("pool", None, "tensor"),
            P("pool", None, "tensor"),
        ),
        check_vma=False,
    )
```

time: 284 us -> 164 us (0.58)
  matrix products: 49.5 us -> 0 us
  waiting for transfers between devices: 97.6 us -> 50.5 us
  local copies, waits for them, and re-layouts: 59 us -> 26 us
  Pallas kernels: 0 us -> 32.9 us
  other arithmetic: 24.9 us -> 9.49 us
  starting transfers between devices: 49.6 us -> 43.1 us
    all_to_all x8 -> x2, waiting for transfers between devices: 97.6 us -> 36.9 us  [the longest x1 36.9 us: local(): got = lax.all_to_all(send, 'pool', split_axis=0, concat_axis=0, tiled=True)]
    dot_general x27 -> x0, matrix products: 49.5 us -> none  [the longest x9 29.3 us: absorb(): jnp.einsum('kgts,skd->kgtd', weights.astype(jnp.bfloat16), values_heads,...]
    gather x2 -> x1, local copies, waits for them, and re-layouts: 45.5 us -> 2.47 us  [local(): my_owners = block_owner[prefix_blocks[me]]]
    pallas_call x0 -> x5, Pallas kernels: none -> 32.9 us  [the longest x1 23.8 us: attend(): pl.pallas_call(attend_kernel, grid=(GROUP,), out_shape=jax.ShapeDtypeStru...]
    all_to_all x8 -> x2, starting transfers between devices: 49.6 us -> 17 us  [the longest x1 12.9 us: local(): got = lax.all_to_all(send, 'pool', split_axis=0, concat_axis=0, tiled=True)]
    ppermute x0 -> x17, starting transfers between devices: none -> 26.1 us  [the longest x7 9.94 us: local(): lax.ppermute(sends[k], 'pool', [(s, (s + PLANE * k) % POOL) for s in rang...]
    reduce_sum x11 -> x2, other arithmetic: 17.2 us -> 0.87 us  [the longest x1 0.78 us: local(): ends = jnp.sum((my_owners[None, :] <= sources[:, None]).astype(i32), axis=1)]
    ppermute x0 -> x17, waiting for transfers between devices: none -> 13.6 us  [the longest x3 5.71 us: local(): lax.ppermute(turned[m], 'pool', [(s, s ^ m) for s in range(POOL)])]
  transfers between devices with their start and end apart: 8 -> 19, of which waited for: 6 -> 8; matrix products, arithmetic and copies ran while one was open for 46% -> 9% of each run, Pallas kernels for 0% -> 3%
where the time goes in v1:
time: 164 us; the launch traced here: 163 us
  waiting for transfers between devices  50.5 us (31%)
  starting transfers between devices  43.1 us (26%)
  Pallas kernels  32.9 us (20%)
  local copies, waits for them, and re-layouts  26 us (16%)
  other arithmetic  9.49 us (6%)
    all_to_all x1, waiting for transfers between devices, local(): got = lax.all_to_all(send, 'pool', split_axis=0, concat_axis=0, tiled=True)  36.9 us
    pallas_call x1, Pallas kernels, attend(): pl.pallas_call(attend_kernel, grid=(GROUP,), out_shape=jax.ShapeDtypeStru...  23.8 us
    unnamed x82, local copies, waits for them, and re-layouts  19.3 us
    all_to_all x1, starting transfers between devices, local(): got = lax.all_to_all(send, 'pool', split_axis=0, concat_axis=0, tiled=True)  12.9 us
    ppermute x7, starting transfers between devices, local(): lax.ppermute(sends[k], 'pool', [(s, (s + PLANE * k) % POOL) for s in rang...  9.94 us
    ppermute x7, starting transfers between devices, local(): piece = lax.ppermute(piece, 'tensor', [(s, s ^ k) for s in range(TENSOR)])  9.89 us
    ppermute x3, starting transfers between devices, local(): lax.ppermute(turned[m], 'pool', [(s, s ^ m) for s in range(POOL)])  6.27 us
    concatenate x8, other arithmetic, local(): jnp.concatenate([lax.dynamic_slice_in_dim(queries, head * GROUP * HD, GRO...  5.74 us
  transfers between devices with their start and end apart: 19, of which 8 were waited for; matrix products, arithmetic and copies ran while one was open for 9% of the time, Pallas kernels for 3%

profile of v1, /device:TPU:1, one launch (start us, length us, event | category | flops | bytes accessed | tf_op | source)
XLA Modules:
  0.0 162.9 jit_solution(10283638753112330089)
XLA Ops:
  5.4 4.2 %pack_blocks.1 = bf16[32,24,16,128]{3,2,1,0:T(8,128)(2,1)} custom-call(s32[1]{0:T(128)} %bitcast.5.me, s32[32,256]{1,0:T(8,128)S(1)} %copy-done.9, s32[64,128]{1,0:T(8,128)S(1)} %bitcast.16, s32[64,128]{1,0:T(8,128)S(1)} %bitcast.18, bf16[256,16,128]{2,1,0:T(8,128)(2,1)S(1)} %copy-done.2, bf16[256,16,128]{2,1,0:T(8,128)(2,1)S(1)} %copy-done.4), custom_call_target="tpu_custom_call" | custom-call | flops 1000000000 | bytes 5000000 | tf_op jit(solution)/shard_map/pack_blocks/pallas_call | solution.py:85
  9.6 12.9 %all-to-all-start = ((bf16[32,24,16,128]{3,2,1,0:T(8,128)(2,1)}), bf16[32,24,16,128]{3,2,1,0:T(8,128)(2,1)S(1)}, u32[]{:S(2)}, u32[]{:S(2)}) async-start(bf16[32,24,16,128]{3,2,1,0:T(8,128)(2,1)} %pack_blocks.1), calls=%async_computation | async-start | bytes 6291456 | tf_op jit(solution)/shard_map/all_to_all | solution.py:322
  22.7 1.8 %constant_dynamic-slice_fusion.2 = (bf16[32,1024]{1,0:T(8,128)(2,1)}, bf16[32,1024]{1,0:T(8,128)(2,1)}, bf16[32,1024]{1,0:T(8,128)(2,1)S(1)}, bf16[32,1024]{1,0:...) fusion(bf16[32,8192]{1,0:T(8,128)(2,1)} %param.10, ...), kind=kLoop, calls=%fused_computation.31 | loop fusion | bytes 1048608 | tf_op jit(solution)/shard_map/dynamic_slice | solution.py:329
  26.9 2.5 %collective-permute-start.1 = (bf16[32,1280]{1,0:T(8,128)(2,1)}, bf16[32,1280]{1,0:T(8,128)(2,1)S(1)}, u32[]{:S(2)}, u32[]{:S(2)}) collective-permute-start(bf16[32,1280]{1,0:T(8,128)(2,1)} %pad_maximum_fusion.2), channel_id=1, source_target_pairs={{0,2},{1,3},{2,0},{3,1},{4,6},{5,7},{6,4},{7,5},{8,10},{9,11},{10,... | collective-permute-start | bytes 245768 | tf_op jit(solution)/shard_map/ppermute | solution.py:336
  32.7 1.3 dynamic_slice.81
  35.3 2.5 %gather_fusion = s32[256]{0:T(256)} fusion(s32[8192]{0:T(1024)S(1)} %copy-done.1, s32[1024]{0:T(1024)} %pad_clamp_fusion), kind=kCustom, calls=%fused_computation | custom fusion | bytes 3072 | tf_op jit(solution)/shard_map/gather | solution.py:340
  42.2 3.9 %collective-permute-start.5 = (bf16[32,1280]{1,0:T(8,128)(2,1)S(1)}, bf16[32,1280]{1,0:T(8,128)(2,1)S(1)}, u32[]{:S(2)}, u32[]{:S(2)}) collective-permute-start(bf16[32,1280]{1,0:T(8,128)(2,1)S(1)} %pad_maximum_fusion.6), channel_id=1, source_target_pairs={{0,6},{1,7},{2,4},{3,5},{4,2},{5,3},{6,0},{7,1},{8,14},{9,15},{10,... | collective-permute-start | bytes 245768 | tf_op jit(solution)/shard_map/ppermute | solution.py:336
  48.3 4.0 %collective-permute-done.6.refs_7_ = bf16[32,1280]{1,0:T(8,128)(2,1)S(1)} collective-permute-done((bf16[32,1280]{1,0:T(8,128)(2,1)S(1)}, bf16[32,1280]{1,0:T(8,128)(2,1)S(1)}, u32[]{:S(2)}, u32[]{:S(2)}) %collective-permute-start.6) | collective-permute-done | bytes 81952 | tf_op jit(solution)/shard_map/ppermute | solution.py:336
  59.6 36.9 %all-to-all-done = bf16[32,24,16,128]{3,2,1,0:T(8,128)(2,1)S(1)} async-done(((bf16[32,24,16,128]{3,2,1,0:T(8,128)(2,1)}), bf16[32,24,16,128]{3,2,1,0:T(8,128)(2,1)S(1)}, u32[]{:S(2)}, u32[]{:S(2)}) %all-to-all-start) | async-done | bytes 3145760 | tf_op jit(solution)/shard_map/all_to_all | solution.py:322
  96.6 1.6 %copy-done.6 = bf16[32,24,16,128]{3,2,1,0:T(8,128)(2,1)} copy-done((bf16[32,24,16,128]{3,2,1,0:T(8,128)(2,1)}, bf16[32,24,16,128]{3,2,1,0:T(8,128)(2,1)S(1)}, u32[]{:S(2)}) %copy-start.6) | copy-done | bytes 3145752
  98.2 1.9 %copy-done.7 = bf16[32,24,16,128]{3,2,1,0:T(8,128)(2,1)S(1)} copy-done((bf16[32,24,16,128]{3,2,1,0:T(8,128)(2,1)S(1)}, bf16[32,24,16,128]{3,2,1,0:T(8,128)(2,1)}, u32[]{:S(2)}) %copy-start.7) | copy-done | bytes 3145752
  102.9 23.8 %attend.1 = bf16[256,1024]{1,0:T(8,128)(2,1)} custom-call(s32[4]{0:T(128)S(1)} %pad_add_fusion.info, s32[256]{0:T(256)S(1)} %add_subtract_fusion.where_from, bf16[8,256,128]{2,1,0:T(8,128)(2,1)S(1)} %copy-done.15, bf16[8,256,128]{2,1,0:T(8,128)(2,1)S(1)} %copy-done.15, bf16[256,128]{1,0:T(8,128)(2,1)S(1)} %copy-done.17, bf16[256,128]{1,0:T(8,128)(2,1)S(1)} %copy-done.19, ...), custom_call_target="tpu_custom_call" | custom-call | flops 8999999488 | bytes 6000000 | tf_op jit(solution)/shard_map/attend/pallas_call | solution.py:277
  126.6 4.1 %all-to-all-start.1 = ((bf16[8,32,1024]{2,1,0:T(8,128)(2,1)}), bf16[8,32,1024]{2,1,0:T(8,128)(2,1)S(1)}, u32[]{:S(2)}, u32[]{:S(2)}) async-start(bf16[8,32,1024]{2,1,0:T(8,128)(2,1)} %bitcast.9), calls=%async_computation.1 | async-start | bytes 1048576 | tf_op jit(solution)/shard_map/all_to_all | solution.py:373
  131.6 1.5 collective-permute-start.9
  133.1 3.7 %collective-permute-start.10 = (bf16[4,2,16,128]{3,2,1,0:T(8,128)(2,1)S(1)}, bf16[4,2,16,128]{3,2,1,0:T(8,128)(2,1)S(1)}, u32[]{:S(2)}, u32[]{:S(2)}) collective-permute-start(bf16[4,2,16,128]{3,2,1,0:T(8,128)(2,1)S(1)} %copy-done.25), channel_id=1, source_target_pairs={{0,128},{8,136},{16,144},{24,152},{32,160},{40,168},{48,176},{56,1... | collective-permute-start | bytes 98312 | tf_op jit(solution)/shard_map/ppermute | solution.py:359
  137.4 2.8 %collective-permute-start.12 = (bf16[4,2,16,128]{3,2,1,0:T(8,128)(2,1)S(1)}, bf16[4,2,16,128]{3,2,1,0:T(8,128)(2,1)S(1)}, u32[]{:S(2)}, u32[]{:S(2)}) collective-permute-start(bf16[4,2,16,128]{3,2,1,0:T(8,128)(2,1)S(1)} %copy-done.21), channel_id=1, source_target_pairs={{0,192},{8,200},{16,208},{24,216},{32,224},{40,232},{48,240},{56,2... | collective-permute-start | bytes 98312 | tf_op jit(solution)/shard_map/ppermute | solution.py:359
  140.8 1.4 collective-permute-done.11.refs_5_
  142.8 1.3 collective-permute-done.13.refs_7_
  144.7 1.6 turn_blocks.1
  146.3 2.9 %collective-permute-start.14 = (bf16[8,2,16,128]{3,2,1,0:T(8,128)(2,1)}, bf16[8,2,16,128]{3,2,1,0:T(8,128)(2,1)S(1)}, u32[]{:S(2)}, u32[]{:S(2)}) collective-permute-start(bf16[8,2,16,128]{3,2,1,0:T(8,128)(2,1)} %get-tuple-element.40), channel_id=1, source_target_pairs={{0,8},{8,0},{16,24},{24,16},{32,40},{40,32},{48,56},{56,48},{64,72... | collective-permute-start | bytes 196616 | tf_op jit(solution)/shard_map/ppermute | solution.py:366
  149.2 3.4 %collective-permute-start.15 = (bf16[8,2,16,128]{3,2,1,0:T(8,128)(2,1)}, bf16[8,2,16,128]{3,2,1,0:T(8,128)(2,1)S(1)}, u32[]{:S(2)}, u32[]{:S(2)}) collective-permute-start(bf16[8,2,16,128]{3,2,1,0:T(8,128)(2,1)} %get-tuple-element.41), channel_id=1, source_target_pairs={{0,16},{8,24},{16,0},{24,8},{32,48},{40,56},{48,32},{56,40},{64,80... | collective-permute-start | bytes 196616 | tf_op jit(solution)/shard_map/ppermute | solution.py:366
  152.6 2.5 %collective-permute-done.15.refs_2_ = bf16[8,2,16,128]{3,2,1,0:T(8,128)(2,1)S(1)} collective-permute-done((bf16[8,2,16,128]{3,2,1,0:T(8,128)(2,1)}, bf16[8,2,16,128]{3,2,1,0:T(8,128)(2,1)S(1)}, u32[]{:S(2)}, u32[]{:S(2)}) %collective-permute-start.15) | collective-permute-done | bytes 65568 | tf_op jit(solution)/shard_map/ppermute | solution.py:366
  155.1 3.2 %collective-permute-done.16.refs_3_ = bf16[8,2,16,128]{3,2,1,0:T(8,128)(2,1)S(1)} collective-permute-done((bf16[8,2,16,128]{3,2,1,0:T(8,128)(2,1)}, bf16[8,2,16,128]{3,2,1,0:T(8,128)(2,1)S(1)}, u32[]{:S(2)}, u32[]{:S(2)}) %collective-permute-start.16) | collective-permute-done | bytes 65568 | tf_op jit(solution)/shard_map/ppermute | solution.py:366
  159.8 2.3 %write_blocks.1 = (bf16[256,16,128]{2,1,0:T(8,128)(2,1)}, bf16[256,16,128]{2,1,0:T(8,128)(2,1)}) custom-call(s32[4]{0:T(128)S(1)} %copy-done.13, s32[32]{0:T(128)S(1)} %get-tuple-element.71.target, bf16[256,16,128]{2,1,0:T(8,128)(2,1)S(1)} %copy-done.3, bf16[256,16,128]{2,1,0:T(8,128)(2,1)S(1)} %copy-done.5, bf16[8,2,16,128]{3,2,1,0:T(8,128)(2,1)S(1)} %copy-done.8, ...), custom_call_target="tpu_custom_call" | custom-call | flops 1000000 | bytes 4000000 | tf_op jit(solution)/shard_map/write_blocks/pallas_call | solution.py:202
  (123 shorter events, 34.1 us)
Async XLA Ops:
  9.6 87.0 %all-to-all-start = ((bf16[32,24,16,128]{3,2,1,0:T(8,128)(2,1)}), bf16[32,24,16,128]{3,2,1,0:T(8,128)(2,1)S(1)}, u32[]{:S(2)}, u32[]{:S(2)}) async-start(bf16[32,24,16,128]{3,2,1,0:T(8,128)(2,1)} %pack_blocks.1), calls=%async_computation | async-start | bytes 6291456 | tf_op jit(solution)/shard_map/all_to_all | solution.py:322
  25.1 17.1 %collective-permute-start = (bf16[32,1280]{1,0:T(8,128)(2,1)}, bf16[32,1280]{1,0:T(8,128)(2,1)S(1)}, u32[]{:S(2)}, u32[]{:S(2)}) collective-permute-start(bf16[32,1280]{1,0:T(8,128)(2,1)} %pad_maximum_fusion.1), channel_id=1, source_target_pairs={{0,1},{1,0},{2,3},{3,2},{4,5},{5,4},{6,7},{7,6},{8,9},{9,8},{10,11... | collective-permute-start | bytes 245768 | tf_op jit(solution)/shard_map/ppermute | solution.py:336
  26.9 19.1 %collective-permute-start.1 = (bf16[32,1280]{1,0:T(8,128)(2,1)}, bf16[32,1280]{1,0:T(8,128)(2,1)S(1)}, u32[]{:S(2)}, u32[]{:S(2)}) collective-permute-start(bf16[32,1280]{1,0:T(8,128)(2,1)} %pad_maximum_fusion.2), channel_id=1, source_target_pairs={{0,2},{1,3},{2,0},{3,1},{4,6},{5,7},{6,4},{7,5},{8,10},{9,11},{10,... | collective-permute-start | bytes 245768 | tf_op jit(solution)/shard_map/ppermute | solution.py:336
  30.0 17.8 %collective-permute-start.2 = (bf16[32,1280]{1,0:T(8,128)(2,1)}, bf16[32,1280]{1,0:T(8,128)(2,1)S(1)}, u32[]{:S(2)}, u32[]{:S(2)}) collective-permute-start(bf16[32,1280]{1,0:T(8,128)(2,1)} %pad_maximum_fusion.3), channel_id=1, source_target_pairs={{0,3},{1,2},{2,1},{3,0},{4,7},{5,6},{6,5},{7,4},{8,11},{9,10},{10,... | collective-permute-start | bytes 245768 | tf_op jit(solution)/shard_map/ppermute | solution.py:336
  30.9 17.0 %collective-permute-start.3 = (bf16[32,1280]{1,0:T(8,128)(2,1)}, bf16[32,1280]{1,0:T(8,128)(2,1)S(1)}, u32[]{:S(2)}, u32[]{:S(2)}) collective-permute-start(bf16[32,1280]{1,0:T(8,128)(2,1)} %pad_maximum_fusion.4), channel_id=1, source_target_pairs={{0,4},{1,5},{2,6},{3,7},{4,0},{5,1},{6,2},{7,3},{8,12},{9,13},{10,... | collective-permute-start | bytes 245768 | tf_op jit(solution)/shard_map/ppermute | solution.py:336
  31.9 15.9 %collective-permute-start.4 = (bf16[32,1280]{1,0:T(8,128)(2,1)}, bf16[32,1280]{1,0:T(8,128)(2,1)}, u32[]{:S(2)}, u32[]{:S(2)}) collective-permute-start(bf16[32,1280]{1,0:T(8,128)(2,1)} %pad_maximum_fusion.5), channel_id=1, source_target_pairs={{0,5},{1,4},{2,7},{3,6},{4,1},{5,0},{6,3},{7,2},{8,13},{9,12},{10,... | collective-permute-start | bytes 245768 | tf_op jit(solution)/shard_map/ppermute | solution.py:336
  42.2 6.1 %collective-permute-start.5 = (bf16[32,1280]{1,0:T(8,128)(2,1)S(1)}, bf16[32,1280]{1,0:T(8,128)(2,1)S(1)}, u32[]{:S(2)}, u32[]{:S(2)}) collective-permute-start(bf16[32,1280]{1,0:T(8,128)(2,1)S(1)} %pad_maximum_fusion.6), channel_id=1, source_target_pairs={{0,6},{1,7},{2,4},{3,5},{4,2},{5,3},{6,0},{7,1},{8,14},{9,15},{10,... | collective-permute-start | bytes 245768 | tf_op jit(solution)/shard_map/ppermute | solution.py:336
  46.1 6.2 %collective-permute-start.6 = (bf16[32,1280]{1,0:T(8,128)(2,1)S(1)}, bf16[32,1280]{1,0:T(8,128)(2,1)S(1)}, u32[]{:S(2)}, u32[]{:S(2)}) collective-permute-start(bf16[32,1280]{1,0:T(8,128)(2,1)S(1)} %pad_maximum_fusion.7), channel_id=1, source_target_pairs={{0,7},{1,6},{2,5},{3,4},{4,3},{5,2},{6,1},{7,0},{8,15},{9,14},{10,... | collective-permute-start | bytes 245768 | tf_op jit(solution)/shard_map/ppermute | solution.py:336
  47.8 78.8 %copy-start.12 = (s32[4]{0:T(128)}, s32[4]{0:T(128)S(1)}, u32[]{:S(2)}) copy-start(s32[4]{0:T(128)S(1)} %pad_add_fusion.info) | copy-start | bytes 52
  102.8 34.0 %copy-start.23 = (bf16[4,2,16,128]{3,2,1,0:T(8,128)(2,1)S(1)}, bf16[4,2,16,128]{3,2,1,0:T(8,128)(2,1)}, u32[]{:S(2)}) copy-start(bf16[4,2,16,128]{3,2,1,0:T(8,128)(2,1)} %copy-done.22) | copy-start | bytes 98308
  102.8 34.5 %copy-start.21 = (bf16[4,2,16,128]{3,2,1,0:T(8,128)(2,1)S(1)}, bf16[4,2,16,128]{3,2,1,0:T(8,128)(2,1)}, u32[]{:S(2)}) copy-start(bf16[4,2,16,128]{3,2,1,0:T(8,128)(2,1)} %copy-done.20) | copy-start | bytes 98308
  102.8 55.5 %copy-start.3 = (bf16[256,16,128]{2,1,0:T(8,128)(2,1)S(1)}, bf16[256,16,128]{2,1,0:T(8,128)(2,1)}, u32[]{:S(2)}) copy-start(bf16[256,16,128]{2,1,0:T(8,128)(2,1)} %keys.3) | copy-start | bytes 3145732
  102.8 55.5 %copy-start.5 = (bf16[256,16,128]{2,1,0:T(8,128)(2,1)S(1)}, bf16[256,16,128]{2,1,0:T(8,128)(2,1)}, u32[]{:S(2)}) copy-start(bf16[256,16,128]{2,1,0:T(8,128)(2,1)} %values.3) | copy-start | bytes 3145732
  126.6 35.5 %all-to-all-start.1 = ((bf16[8,32,1024]{2,1,0:T(8,128)(2,1)}), bf16[8,32,1024]{2,1,0:T(8,128)(2,1)S(1)}, u32[]{:S(2)}, u32[]{:S(2)}) async-start(bf16[8,32,1024]{2,1,0:T(8,128)(2,1)} %bitcast.9), calls=%async_computation.1 | async-start | bytes 1048576 | tf_op jit(solution)/shard_map/all_to_all | solution.py:373
  130.8 6.6 %collective-permute-start.7 = (bf16[4,2,16,128]{3,2,1,0:T(8,128)(2,1)S(1)}, bf16[4,2,16,128]{3,2,1,0:T(8,128)(2,1)S(1)}, u32[]{:S(2)}, u32[]{:S(2)}) collective-permute-start(bf16[4,2,16,128]{3,2,1,0:T(8,128)(2,1)S(1)} %copy-done.31), channel_id=1, source_target_pairs={{0,32},{8,40},{16,48},{24,56},{32,64},{40,72},{48,80},{56,88},{64,... | collective-permute-start | bytes 98312 | tf_op jit(solution)/shard_map/ppermute | solution.py:359
  130.9 9.3 %collective-permute-start.8 = (bf16[4,2,16,128]{3,2,1,0:T(8,128)(2,1)S(1)}, bf16[4,2,16,128]{3,2,1,0:T(8,128)(2,1)S(1)}, u32[]{:S(2)}, u32[]{:S(2)}) collective-permute-start(bf16[4,2,16,128]{3,2,1,0:T(8,128)(2,1)S(1)} %copy-done.29), channel_id=1, source_target_pairs={{0,64},{8,72},{16,80},{24,88},{32,96},{40,104},{48,112},{56,120},{... | collective-permute-start | bytes 98312 | tf_op jit(solution)/shard_map/ppermute | solution.py:359
  131.6 9.1 %collective-permute-start.9 = (bf16[4,2,16,128]{3,2,1,0:T(8,128)(2,1)S(1)}, bf16[4,2,16,128]{3,2,1,0:T(8,128)(2,1)S(1)}, u32[]{:S(2)}, u32[]{:S(2)}) collective-permute-start(bf16[4,2,16,128]{3,2,1,0:T(8,128)(2,1)S(1)} %copy-done.27), channel_id=1, source_target_pairs={{0,96},{8,104},{16,112},{24,120},{32,128},{40,136},{48,144},{56,15... | collective-permute-start | bytes 98312 | tf_op jit(solution)/shard_map/ppermute | solution.py:359
  133.1 7.7 %collective-permute-start.10 = (bf16[4,2,16,128]{3,2,1,0:T(8,128)(2,1)S(1)}, bf16[4,2,16,128]{3,2,1,0:T(8,128)(2,1)S(1)}, u32[]{:S(2)}, u32[]{:S(2)}) collective-permute-start(bf16[4,2,16,128]{3,2,1,0:T(8,128)(2,1)S(1)} %copy-done.25), channel_id=1, source_target_pairs={{0,128},{8,136},{16,144},{24,152},{32,160},{40,168},{48,176},{56,1... | collective-permute-start | bytes 98312 | tf_op jit(solution)/shard_map/ppermute | solution.py:359
  136.8 5.4 %collective-permute-start.11 = (bf16[4,2,16,128]{3,2,1,0:T(8,128)(2,1)S(1)}, bf16[4,2,16,128]{3,2,1,0:T(8,128)(2,1)S(1)}, u32[]{:S(2)}, u32[]{:S(2)}) collective-permute-start(bf16[4,2,16,128]{3,2,1,0:T(8,128)(2,1)S(1)} %copy-done.23), channel_id=1, source_target_pairs={{0,160},{8,168},{16,176},{24,184},{32,192},{40,200},{48,208},{56,2... | collective-permute-start | bytes 98312 | tf_op jit(solution)/shard_map/ppermute | solution.py:359
  137.4 5.5 %collective-permute-start.12 = (bf16[4,2,16,128]{3,2,1,0:T(8,128)(2,1)S(1)}, bf16[4,2,16,128]{3,2,1,0:T(8,128)(2,1)S(1)}, u32[]{:S(2)}, u32[]{:S(2)}) collective-permute-start(bf16[4,2,16,128]{3,2,1,0:T(8,128)(2,1)S(1)} %copy-done.21), channel_id=1, source_target_pairs={{0,192},{8,200},{16,208},{24,216},{32,224},{40,232},{48,240},{56,2... | collective-permute-start | bytes 98312 | tf_op jit(solution)/shard_map/ppermute | solution.py:359
  140.2 3.9 %collective-permute-start.13 = (bf16[4,2,16,128]{3,2,1,0:T(8,128)(2,1)S(1)}, bf16[4,2,16,128]{3,2,1,0:T(8,128)(2,1)S(1)}, u32[]{:S(2)}, u32[]{:S(2)}) collective-permute-start(bf16[4,2,16,128]{3,2,1,0:T(8,128)(2,1)S(1)} %get-tuple-element.38), channel_id=1, source_target_pairs={{0,224},{8,232},{16,240},{24,248},{32,0},{40,8},{48,16},{56,24},{6... | collective-permute-start | bytes 98312 | tf_op jit(solution)/shard_map/ppermute | solution.py:359
  146.3 6.3 %collective-permute-start.14 = (bf16[8,2,16,128]{3,2,1,0:T(8,128)(2,1)}, bf16[8,2,16,128]{3,2,1,0:T(8,128)(2,1)S(1)}, u32[]{:S(2)}, u32[]{:S(2)}) collective-permute-start(bf16[8,2,16,128]{3,2,1,0:T(8,128)(2,1)} %get-tuple-element.40), channel_id=1, source_target_pairs={{0,8},{8,0},{16,24},{24,16},{32,40},{40,32},{48,56},{56,48},{64,72... | collective-permute-start | bytes 196616 | tf_op jit(solution)/shard_map/ppermute | solution.py:366
  149.2 6.0 %collective-permute-start.15 = (bf16[8,2,16,128]{3,2,1,0:T(8,128)(2,1)}, bf16[8,2,16,128]{3,2,1,0:T(8,128)(2,1)S(1)}, u32[]{:S(2)}, u32[]{:S(2)}) collective-permute-start(bf16[8,2,16,128]{3,2,1,0:T(8,128)(2,1)} %get-tuple-element.41), channel_id=1, source_target_pairs={{0,16},{8,24},{16,0},{24,8},{32,48},{40,56},{48,32},{56,40},{64,80... | collective-permute-start | bytes 196616 | tf_op jit(solution)/shard_map/ppermute | solution.py:366
  152.6 5.8 %collective-permute-start.16 = (bf16[8,2,16,128]{3,2,1,0:T(8,128)(2,1)}, bf16[8,2,16,128]{3,2,1,0:T(8,128)(2,1)S(1)}, u32[]{:S(2)}, u32[]{:S(2)}) collective-permute-start(bf16[8,2,16,128]{3,2,1,0:T(8,128)(2,1)} %get-tuple-element.42), channel_id=1, source_target_pairs={{0,24},{8,16},{16,8},{24,0},{32,56},{40,48},{48,40},{56,32},{64,88... | collective-permute-start | bytes 196616 | tf_op jit(solution)/shard_map/ppermute | solution.py:366
  (36 other events, 207.1 us)

commit v2 on v1

v2 whole, which is shorter than its diff:
```python
import jax
import jax.numpy as jnp
from jax import lax
from jax.experimental import pallas as pl
from jax.experimental.pallas import tpu as pltpu
from jax.sharding import PartitionSpec as P

H = 64
KVH = 8
HD = 128
GROUP = H // KVH
BLK = 16
POOL = 32
TENSOR = 8
SLOTS = 256
PBLK = 256
CAP = 12
TOK = 256
NEWB = TOK // BLK
LOAD = 2 * CAP
PART = 8
WIDE = 60 * 1024 * 1024
SCALE = HD ** (-0.5) * 1.4426950408889634
neg_big = -1e30

bf16 = jnp.bfloat16
f32 = jnp.float32
i32 = jnp.int32

VMEM = pl.BlockSpec(memory_space=pltpu.VMEM)
SMEM = pl.BlockSpec(memory_space=pltpu.SMEM)
HBM = pl.BlockSpec(memory_space=pltpu.HBM)
NT = (((1,), (1,)), ((), ()))


def cost(flops, moved, exps=0):
    return pl.CostEstimate(flops=flops, bytes_accessed=moved, transcendentals=exps)


def pack_kernel(me, prefix_h, owner_h, slot_h, keys_h, values_h, out_h, *scratch):
    prefix, owner, slot, keys, values, wanted, picked, picked_s, out, sems, out_sems = scratch
    sources = (prefix_h, owner_h, slot_h, keys_h, values_h)
    copies = [
        pltpu.make_async_copy(source, target, sems.at[i])
        for i, (source, target) in enumerate(zip(sources, scratch[:5]))
    ]
    for copy in copies:
        copy.start()
    for copy in copies[:3]:
        copy.wait()
    rows, lanes = owner.shape
    mine = jnp.where(owner[...] == me[0], slot[...] + 1, 0).astype(f32).astype(bf16)
    lane_of = lax.broadcasted_iota(i32, (lanes, PBLK), 0)
    row_of = lax.broadcasted_iota(i32, (rows, PBLK), 0)
    for g in range(POOL):
        index = prefix[g : g + 1, :]
        low = index & (lanes - 1)
        high = index >> 7
        hot = jnp.where(lane_of == low, 1.0, 0.0).astype(bf16)
        found = jnp.dot(mine, hot, preferred_element_type=f32)
        wanted[g : g + 1, :] = jnp.sum(
            jnp.where(row_of == high, found, 0.0), axis=0, keepdims=True
        )
    place = wanted[...]
    held = place > 0.5
    before = lax.broadcasted_iota(i32, (PBLK, PBLK), 0)
    after = lax.broadcasted_iota(i32, (PBLK, PBLK), 1)
    triangle = jnp.where(before <= after, 1.0, 0.0).astype(bf16)
    rank = jnp.dot(
        jnp.where(held, 1.0, 0.0).astype(bf16), triangle, preferred_element_type=f32
    )
    rank = jnp.where(held, rank, 0.0)
    lane = lax.broadcasted_iota(i32, (POOL, 128), 1)
    chosen = jnp.zeros((POOL, 128), f32)
    for r in range(CAP):
        one = jnp.sum(jnp.where(rank == r + 1.0, place - 1.0, 0.0), axis=1, keepdims=True)
        chosen = jnp.where(lane == r, one, chosen)
    picked[...] = chosen.astype(i32)
    listed = pltpu.make_async_copy(picked, picked_s, sems.at[5])
    listed.start()
    listed.wait()
    for copy in copies[3:]:
        copy.wait()

    leaving = []
    for part in range(POOL // PART):
        groups = pl.ds(part * PART, PART)

        @pl.loop(part * PART, (part + 1) * PART)
        def _(g):
            for r in range(CAP):
                s = picked_s[g, r]
                out[g, r] = keys[s]
                out[g, CAP + r] = values[s]

        leaving.append(
            pltpu.make_async_copy(out.at[groups], out_h.at[groups], out_sems.at[part])
        )
        leaving[-1].start()
    for copy in leaving:
        copy.wait()


def pack(me, prefix_blocks, block_owner, block_slot, pool_keys, pool_values):
    table = (block_owner.shape[0] // 128, 128)
    return pl.pallas_call(
        pack_kernel,
        out_shape=jax.ShapeDtypeStruct((POOL, LOAD, BLK, HD), bf16),
        in_specs=[SMEM] + [HBM] * 5,
        out_specs=HBM,
        scratch_shapes=[
            pltpu.VMEM(prefix_blocks.shape, i32),
            pltpu.VMEM(table, i32),
            pltpu.VMEM(table, i32),
            pltpu.VMEM(pool_keys.shape, bf16),
            pltpu.VMEM(pool_values.shape, bf16),
            pltpu.VMEM((POOL, PBLK), f32),
            pltpu.VMEM((POOL, 128), i32),
            pltpu.SMEM((POOL, 128), i32),
            pltpu.VMEM((POOL, LOAD, BLK, HD), bf16),
            pltpu.SemaphoreType.DMA((6,)),
            pltpu.SemaphoreType.DMA((POOL // PART,)),
        ],
        compiler_params=pltpu.CompilerParams(vmem_limit_bytes=WIDE),
        cost_estimate=cost(10**9, 5 * 10**6),
        name="pack_blocks",
    )(
        me.reshape(1),
        prefix_blocks,
        block_owner.reshape(table),
        block_slot.reshape(table),
        pool_keys,
        pool_values,
    )


def gather_kernel(info, evict, *refs):
    pieces = refs[:TENSOR]
    heads, shift, start, sends, own_keys, own_values = refs[TENSOR:]
    t, count, me = info[0], info[1], info[2]
    rows = TOK // TENSOR
    for k in range(TENSOR):
        begin = pl.multiple_of((t ^ k) * rows, rows)
        at = pl.ds(begin, rows)
        for h in range(GROUP):
            heads[pl.ds(pl.multiple_of(h * TOK + begin, rows), rows), :] = pieces[k][
                :, h * HD : (h + 1) * HD
            ]
        own_keys[at, :] = pieces[k][:, GROUP * HD : (GROUP + 1) * HD]
        own_values[at, :] = pieces[k][:, (GROUP + 1) * HD :]
    place = lax.broadcasted_iota(i32, (BLK, HD), 0)
    for j in range(NEWB):
        owner = evict[me, j] >> 8
        live = j * BLK + place < count
        for part, own in enumerate((own_keys, own_values)):
            block = own[j * BLK : (j + 1) * BLK, :]
            sends[owner, part] = jnp.where(live, block.astype(f32), 0.0).astype(bf16)
    both = jnp.concatenate([own_values[...], jnp.ones((TOK, HD), bf16)], axis=1)
    row = lax.broadcasted_iota(i32, (TOK, TOK), 0)
    column = lax.broadcasted_iota(i32, (TOK, TOK), 1)

    @pl.loop(0, GROUP)
    def _(h):
        at = pl.ds(pl.multiple_of(h * TOK, TOK), TOK)
        scores = lax.dot_general(heads[at, :], own_keys[...], NT, preferred_element_type=f32)
        scores = jnp.where(column <= row, scores * SCALE, neg_big)
        top = jnp.max(scores, axis=1, keepdims=True)
        shift[at, :] = jnp.broadcast_to(top, (TOK, HD))
        weights = jnp.exp2(scores - top).astype(bf16)
        start[at, :] = jnp.dot(weights, both, preferred_element_type=f32)


def gather(info, evict_slots, pieces):
    return pl.pallas_call(
        gather_kernel,
        out_shape=[
            jax.ShapeDtypeStruct((GROUP * TOK, HD), bf16),
            jax.ShapeDtypeStruct((GROUP * TOK, HD), f32),
            jax.ShapeDtypeStruct((GROUP * TOK, 2 * HD), f32),
            jax.ShapeDtypeStruct((POOL, 2, BLK, HD), bf16),
        ],
        in_specs=[SMEM, SMEM] + [VMEM] * TENSOR,
        out_specs=[VMEM] * 4,
        scratch_shapes=[pltpu.VMEM((TOK, HD), bf16), pltpu.VMEM((TOK, HD), bf16)],
        compiler_params=pltpu.CompilerParams(vmem_limit_bytes=16 * 1024 * 1024),
        cost_estimate=cost(10**9, 4 * 10**6),
        name="gather_rows",
    )(info, evict_slots, *pieces)


def write_kernel(target, keys, values, arrived, out_keys, out_values):
    out_keys[...] = keys[...]
    out_values[...] = values[...]
    for g in range(POOL):
        slot = target[g]

        @pl.when(slot >= 0)
        def _():
            out_keys[slot] = arrived[g, 0]
            out_values[slot] = arrived[g, 1]


def write(target, pool_keys, pool_values, arrived):
    return pl.pallas_call(
        write_kernel,
        out_shape=[jax.ShapeDtypeStruct(pool_keys.shape, bf16)] * 2,
        in_specs=[SMEM] + [VMEM] * 3,
        out_specs=[VMEM] * 2,
        compiler_params=pltpu.CompilerParams(vmem_limit_bytes=16 * 1024 * 1024),
        cost_estimate=cost(10**6, 4 * 10**6),
        name="write_blocks",
    )(target, pool_keys, pool_values, arrived)


KEYS = PBLK * BLK
ROWS = 1024
TILE = 256
SMALL = 256


def attend_kernel(
    info, where_from, heads_h, shift_h, start_h, got, out, keys, values, heads, shift, start, sems
):
    copies = [
        pltpu.make_async_copy(source, target, sems.at[i])
        for i, (source, target) in enumerate(
            [(heads_h, heads), (shift_h, shift), (start_h, start)]
        )
    ]
    for copy in copies:
        copy.start()
    for b in range(PBLK):
        index = where_from[b]
        keys[b * BLK : (b + 1) * BLK, :] = got[index]
        values[b * BLK : (b + 1) * BLK, :] = got[index + CAP]
    for copy in copies:
        copy.wait()
    ones = jnp.ones((TILE, HD), bf16)
    live = lax.broadcasted_iota(i32, (TOK, HD), 0) < info[1]

    def finish(h, summed):
        result = summed[:, :HD] / summed[:, HD:]
        out[:, h * HD : (h + 1) * HD] = jnp.where(live, result, 0.0).astype(bf16)

    for i in range(GROUP * TOK // ROWS):
        query = heads[i * ROWS : (i + 1) * ROWS, :]
        top = shift[i * ROWS : (i + 1) * ROWS, :]
        summed = start[i * ROWS : (i + 1) * ROWS, :]
        for j in range(KEYS // TILE):
            tile = slice(j * TILE, (j + 1) * TILE)
            part = lax.dot_general(query, keys[tile, :], NT, preferred_element_type=f32)
            weights = jnp.concatenate(
                [
                    jnp.exp2(part[:, c * HD : (c + 1) * HD] * SCALE - top)
                    for c in range(TILE // HD)
                ],
                axis=1,
            ).astype(bf16)
            both = jnp.concatenate([values[tile, :], ones], axis=1)
            summed = summed + jnp.dot(weights, both, preferred_element_type=f32)
        for h in range(ROWS // TOK):
            finish(i * (ROWS // TOK) + h, summed[h * TOK : (h + 1) * TOK, :])
        largest = jnp.max(summed[:, HD:])

        @pl.when(jnp.logical_not(largest < 1e30))
        def _():
            for h in range(ROWS // TOK):
                at = slice(i * ROWS + h * TOK, i * ROWS + (h + 1) * TOK)

                def one(j, state):
                    best, summed = state
                    tile = pl.ds(pl.multiple_of(j * SMALL, SMALL), SMALL)
                    part = (
                        lax.dot_general(
                            heads[at, :], keys[tile, :], NT, preferred_element_type=f32
                        )
                        * SCALE
                    )
                    above = jnp.maximum(best, jnp.max(part, axis=1, keepdims=True))
                    weights = jnp.exp2(part - above).astype(bf16)
                    both = jnp.concatenate([values[tile, :], ones], axis=1)
                    summed = summed * jnp.exp2(best - above) + jnp.dot(
                        weights, both, preferred_element_type=f32
                    )
                    return above, summed

                best, summed = lax.fori_loop(
                    0, KEYS // SMALL, one, (shift[at, :1], start[at, :])
                )
                finish(i * (ROWS // TOK) + h, summed)


def attend(info, where_from, heads, shift, start, got):
    blocks = got.shape[0] * got.shape[1]
    return pl.pallas_call(
        attend_kernel,
        out_shape=jax.ShapeDtypeStruct((TOK, GROUP * HD), bf16),
        in_specs=[SMEM, SMEM] + [HBM] * 3 + [VMEM],
        out_specs=VMEM,
        scratch_shapes=[
            pltpu.VMEM((KEYS, HD), bf16),
            pltpu.VMEM((KEYS, HD), bf16),
            pltpu.VMEM(heads.shape, bf16),
            pltpu.VMEM(shift.shape, f32),
            pltpu.VMEM(start.shape, f32),
            pltpu.SemaphoreType.DMA((3,)),
        ],
        compiler_params=pltpu.CompilerParams(vmem_limit_bytes=57 * 1024 * 1024),
        cost_estimate=cost(9 * 10**9, 6 * 10**6, 9 * 10**6),
        name="attend",
    )(info, where_from, heads, shift, start, got.reshape(blocks, BLK, HD))


def local(
    queries,
    new_keys,
    new_values,
    pool_keys,
    pool_values,
    prefix_blocks,
    block_owner,
    block_slot,
    evict_slots,
    tok_counts,
):
    me = lax.axis_index("pool").astype(i32)
    t = lax.axis_index("tensor").astype(i32)
    share = TOK // TENSOR
    info = jnp.stack([t, tok_counts[me], me])

    send = pack(me, prefix_blocks, block_owner, block_slot, pool_keys, pool_values)
    send, queries, new_keys, new_values = lax.optimization_barrier(
        (send, queries, new_keys, new_values)
    )
    got = lax.all_to_all(send, "pool", split_axis=0, concat_axis=0, tiled=True)

    pieces = []
    for k in range(TENSOR):
        head = t ^ k
        piece = jnp.concatenate(
            [
                lax.dynamic_slice_in_dim(queries, head * GROUP * HD, GROUP * HD, 1),
                lax.dynamic_slice_in_dim(new_keys, head * HD, HD, 1),
                lax.dynamic_slice_in_dim(new_values, head * HD, HD, 1),
            ],
            axis=1,
        )
        if k:
            piece = lax.ppermute(piece, "tensor", [(s, s ^ k) for s in range(TENSOR)])
        pieces.append(piece)

    sources = jnp.arange(POOL, dtype=i32)
    my_owners = block_owner[prefix_blocks[me]]
    ends = jnp.sum((my_owners[None, :] <= sources[:, None]).astype(i32), axis=1)
    starts = jnp.sum((my_owners[None, :] < sources[:, None]).astype(i32), axis=1)
    nth = jnp.arange(PBLK, dtype=i32)
    which = jnp.sum((ends[None, :] <= nth[:, None]).astype(i32), axis=1)
    base = jnp.max(jnp.where(starts[None, :] <= nth[:, None], starts[None, :], 0), axis=1)
    where_from = which * LOAD + nth - base

    target = jnp.max(jnp.where(evict_slots // SLOTS == me, evict_slots % SLOTS, -1), axis=1)

    heads, shift, start, sends = gather(info, evict_slots, pieces)
    got, sends = lax.optimization_barrier((got, sends))
    arrived = lax.all_to_all(sends, "pool", split_axis=0, concat_axis=0, tiled=True)
    result = attend(info, where_from, heads, shift, start, got)
    result, arrived = lax.optimization_barrier((result, arrived))
    result = result.reshape(TENSOR, share, GROUP * HD)
    attended = lax.all_to_all(result, "tensor", split_axis=0, concat_axis=0, tiled=True)
    attended = jnp.transpose(attended, (1, 0, 2)).reshape(share, H * HD)
    new_pool_keys, new_pool_values = write(target, pool_keys, pool_values, arrived)
    return (attended, new_pool_keys, new_pool_values)


def solution(mesh):
    placed = (
        P(("pool", "tensor"), None),
        P(("pool", "tensor"), None),
        P(("pool", "tensor"), None),
        P("pool", None, "tensor"),
        P("pool", None, "tensor"),
        P(),
        P(),
        P(),
        P(),
        P(),
    )
    return jax.shard_map(
        local,
        mesh=mesh,
        in_specs=placed,
        out_specs=(
            P(("pool", "tensor"), None),
            P("pool", None, "tensor"),
            P("pool", None, "tensor"),
        ),
        check_vma=False,
    )
```

time: 164 us -> 203 us (1.24)
  Pallas kernels: 32.9 us -> 101 us
  local copies, waits for them, and re-layouts: 26 us -> 6.49 us
  starting transfers between devices: 43.1 us -> 33.1 us
  waiting for transfers between devices: 50.5 us -> 59.2 us
  other arithmetic: 9.49 us -> 2.28 us
    pallas_call x4 -> x3, Pallas kernels: 30.6 us -> 98.4 us  [the longest x1 89.2 us: attend(): pl.pallas_call(attend_kernel, out_shape=jax.ShapeDtypeStruct((TOK, GROUP...]
    ppermute x10 -> x0, starting transfers between devices: 16.2 us -> none  [the longest x7 9.94 us: local(): lax.ppermute(sends[k], 'pool', [(s, (s + PLANE * k) % POOL) for s in rang...]
    unnamed x82 -> x25, local copies, waits for them, and re-layouts: 19.3 us -> 3.24 us
    all_to_all x1, waiting for transfers between devices: 36.9 us -> 46.5 us  [local(): got = lax.all_to_all(send, 'pool', split_axis=0, concat_axis=0, tiled=True)]
    ppermute x10 -> x0, waiting for transfers between devices: 9.1 us -> none  [the longest x3 5.71 us: local(): lax.ppermute(turned[m], 'pool', [(s, s ^ m) for s in range(POOL)])]
    all_to_all x1, waiting for transfers between devices: 0.01 us -> 7.95 us  [local(): lax.all_to_all(result, 'tensor', split_axis=0, concat_axis=0, tiled=True)]
    all_to_all x0 -> x1, starting transfers between devices: none -> 6.15 us  [local(): lax.all_to_all(sends, 'pool', split_axis=0, concat_axis=0, tiled=True)]
    concatenate x8, other arithmetic: 5.74 us -> 0.07 us  [local(): jnp.concatenate([lax.dynamic_slice_in_dim(queries, head * GROUP * HD, GRO...]
  transfers between devices with their start and end apart: 19 -> 10, of which waited for: 8 -> 4; matrix products, arithmetic and copies ran while one was open for 9% -> 2% of each run, Pallas kernels for 3% -> 47%
where the time goes in v2:
time: 203 us
  Pallas kernels  101 us (50%)
  waiting for transfers between devices  59.2 us (29%)
  starting transfers between devices  33.1 us (16%)
  local copies, waits for them, and re-layouts  6.49 us (3%)
  other arithmetic  2.28 us (1%)
    pallas_call x1, Pallas kernels, attend(): pl.pallas_call(attend_kernel, out_shape=jax.ShapeDtypeStruct((TOK, GROUP...  89.2 us
    all_to_all x1, waiting for transfers between devices, local(): got = lax.all_to_all(send, 'pool', split_axis=0, concat_axis=0, tiled=True)  46.5 us
    all_to_all x1, starting transfers between devices, local(): got = lax.all_to_all(send, 'pool', split_axis=0, concat_axis=0, tiled=True)  12.9 us
    ppermute x7, starting transfers between devices, local(): piece = lax.ppermute(piece, 'tensor', [(s, s ^ k) for s in range(TENSOR)])  10.2 us
    all_to_all x1, waiting for transfers between devices, local(): lax.all_to_all(result, 'tensor', split_axis=0, concat_axis=0, tiled=True)  7.95 us
    all_to_all x1, starting transfers between devices, local(): lax.all_to_all(sends, 'pool', split_axis=0, concat_axis=0, tiled=True)  6.15 us
    ppermute x7, waiting for transfers between devices, local(): piece = lax.ppermute(piece, 'tensor', [(s, s ^ k) for s in range(TENSOR)])  4.76 us
    pallas_call x1, Pallas kernels, gather(): pl.pallas_call(gather_kernel, out_shape=[jax.ShapeDtypeStruct((GROUP * TO...  4.6 us
  transfers between devices with their start and end apart: 10, of which 4 were waited for; matrix products, arithmetic and copies ran while one was open for 2% of the time, Pallas kernels for 47%

profile of v2, /device:TPU:1, one launch (start us, length us, event | category | flops | bytes accessed | tf_op | source)
XLA Modules:
  0.0 202.7 jit_solution(11345445406184123066)
XLA Ops:
  0.6 4.6 %pack_blocks.1 = bf16[32,24,16,128]{3,2,1,0:T(8,128)(2,1)} custom-call(s32[1]{0:T(128)} %bitcast.1.me, s32[32,256]{1,0:T(8,128)} %prefix_h.1, s32[64,128]{1,0:T(8,128)} %bitcast.14, s32[64,128]{1,0:T(8,128)} %bitcast.18, bf16[256,16,128]{2,1,0:T(8,128)(2,1)} %keys.1, bf16[256,16,128]{2,1,0:T(8,128)(2,1)} %values.1), custom_call_target="tpu_custom_call" | custom-call | flops 1000000000 | bytes 5000000 | tf_op jit(solution)/shard_map/pack_blocks/pallas_call | solution.py:106
  5.3 12.9 %all-to-all-start = ((bf16[32,24,16,128]{3,2,1,0:T(8,128)(2,1)}), bf16[32,24,16,128]{3,2,1,0:T(8,128)(2,1)}, u32[]{:S(2)}, u32[]{:S(2)}) async-start(bf16[32,24,16,128]{3,2,1,0:T(8,128)(2,1)} %pack_blocks.1), calls=%async_computation | async-start | bytes 6291456 | tf_op jit(solution)/shard_map/all_to_all | solution.py:335
  18.5 1.3 collective-permute-start
  19.8 2.5 %collective-permute-start.1 = (bf16[32,1280]{1,0:T(8,128)(2,1)S(1)}, bf16[32,1280]{1,0:T(8,128)(2,1)S(1)}, u32[]{:S(2)}, u32[]{:S(2)}) collective-permute-start(bf16[32,1280]{1,0:T(8,128)(2,1)S(1)} %pad_maximum_fusion.2), channel_id=1, source_target_pairs={{0,2},{1,3},{2,0},{3,1},{4,6},{5,7},{6,4},{7,5},{8,10},{9,11},{10,... | collective-permute-start | bytes 245768 | tf_op jit(solution)/shard_map/ppermute | solution.py:349
  23.1 0.9 collective-permute-start.4
  24.0 0.7 compare_select_fusion
  24.7 1.7 gather_fusion
  27.3 0.6 dynamic_slice.78
  27.9 3.8 %collective-permute-start.5 = (bf16[32,1280]{1,0:T(8,128)(2,1)S(1)}, bf16[32,1280]{1,0:T(8,128)(2,1)S(1)}, u32[]{:S(2)}, u32[]{:S(2)}) collective-permute-start(bf16[32,1280]{1,0:T(8,128)(2,1)S(1)} %pad_maximum_fusion.6), channel_id=1, source_target_pairs={{0,6},{1,7},{2,4},{3,5},{4,2},{5,3},{6,0},{7,1},{8,14},{9,15},{10,... | collective-permute-start | bytes 245768 | tf_op jit(solution)/shard_map/ppermute | solution.py:349
  31.7 1.0 collective-permute-start.6
  32.7 0.7 pad_add_fusion.info
  33.5 0.7 collective-permute-done.5.refs_6_
  34.1 4.1 %collective-permute-done.6.refs_7_ = bf16[32,1280]{1,0:T(8,128)(2,1)S(1)} collective-permute-done((bf16[32,1280]{1,0:T(8,128)(2,1)S(1)}, bf16[32,1280]{1,0:T(8,128)(2,1)S(1)}, u32[]{:S(2)}, u32[]{:S(2)}) %collective-permute-start.6) | collective-permute-done | bytes 81952 | tf_op jit(solution)/shard_map/ppermute | solution.py:349
  38.2 4.6 %gather_rows.1 = (bf16[2048,128]{1,0:T(8,128)(2,1)S(1)}, f32[2048,128]{1,0:T(8,128)S(1)}, f32[2048,256]{1,0:T(8,128)S(1)}, bf16[32,2,16,128]{3,2,1,0:T(8,128)(2,1)}) custom-call(s32[3]{0:T(128)S(1)} %pad_add_fusion.info, s32[32,16]{1,0:T(8,128)S(1)} %copy.17.evict, bf16[32,1280]{1,0:T(8,128)(2,1)S(1)} %pad_maximum_fusion.refs_0_, ...), custom_call_target="tpu_custom_call" | custom-call | flops 1000000000 | bytes 4000000 | tf_op jit(solution)/shard_map/gather_rows/pallas_call | solution.py:174
  42.8 1.4 copy-done.3
  44.2 1.0 copy-done.4
  45.1 0.8 copy-done.5
  45.9 46.5 %all-to-all-done = bf16[32,24,16,128]{3,2,1,0:T(8,128)(2,1)} async-done(((bf16[32,24,16,128]{3,2,1,0:T(8,128)(2,1)}), bf16[32,24,16,128]{3,2,1,0:T(8,128)(2,1)}, u32[]{:S(2)}, u32[]{:S(2)}) %all-to-all-start) | async-done | bytes 3145760 | tf_op jit(solution)/shard_map/all_to_all | solution.py:335
  92.4 6.1 %all-to-all-start.1 = ((bf16[32,2,16,128]{3,2,1,0:T(8,128)(2,1)}), bf16[32,2,16,128]{3,2,1,0:T(8,128)(2,1)S(1)}, u32[]{:S(2)}, u32[]{:S(2)}) async-start(bf16[32,2,16,128]{3,2,1,0:T(8,128)(2,1)} %get-tuple-element.26), calls=%async_computation.1 | async-start | bytes 524288 | tf_op jit(solution)/shard_map/all_to_all | solution.py:365
  98.6 89.2 %attend.1 = bf16[256,1024]{1,0:T(8,128)(2,1)} custom-call(s32[3]{0:T(128)} %copy-done.2, s32[256]{0:T(256)} %add_subtract_fusion.where_from, bf16[2048,128]{1,0:T(8,128)(2,1)} %copy-done.5, f32[2048,128]{1,0:T(8,128)} %copy-done.4, f32[2048,256]{1,0:T(8,128)} %copy-done.3, bf16[768,16,128]{2,1,0:T(8,128)(2,1)} %bitcast.6.got), custom_call_target="tpu_custom_call" | custom-call | flops 8999999488 | bytes 6000000 | tf_op jit(solution)/shard_map/attend/pallas_call | solution.py:295
  187.9 3.8 %all-to-all-start.2 = ((bf16[8,32,1024]{2,1,0:T(8,128)(2,1)}), bf16[8,32,1024]{2,1,0:T(8,128)(2,1)S(1)}, u32[]{:S(2)}, u32[]{:S(2)}) async-start(bf16[8,32,1024]{2,1,0:T(8,128)(2,1)} %bitcast.16), calls=%async_computation.2 | async-start | bytes 1048576 | tf_op jit(solution)/shard_map/all_to_all | solution.py:369
  191.7 2.2 %write_blocks.1 = (bf16[256,16,128]{2,1,0:T(8,128)(2,1)}, bf16[256,16,128]{2,1,0:T(8,128)(2,1)}) custom-call(s32[32]{0:T(128)S(1)} %fusion.2.target, bf16[256,16,128]{2,1,0:T(8,128)(2,1)S(1)} %copy-done, bf16[256,16,128]{2,1,0:T(8,128)(2,1)S(1)} %copy-done.1, bf16[32,2,16,128]{3,2,1,0:T(8,128)(2,1)S(1)} %all-to-all-done.1.arrived), custom_call_target="tpu_custom_call" | custom-call | flops 1000000 | bytes 4000000 | tf_op jit(solution)/shard_map/write_blocks/pallas_call | solution.py:204
  193.9 8.0 %all-to-all-done.2 = bf16[8,32,1024]{2,1,0:T(8,128)(2,1)S(1)} async-done(((bf16[8,32,1024]{2,1,0:T(8,128)(2,1)}), bf16[8,32,1024]{2,1,0:T(8,128)(2,1)S(1)}, u32[]{:S(2)}, u32[]{:S(2)}) %all-to-all-start.2) | async-done | bytes 524320 | tf_op jit(solution)/shard_map/all_to_all | solution.py:369
  201.9 0.8 copy.19
  (45 shorter events, 1.9 us)
Async XLA Ops:
  5.2 13.1 %copy-start.8 = (bf16[32,1024]{1,0:T(8,128)(2,1)S(1)}, bf16[32,1024]{1,0:T(8,128)(2,1)}, u32[]{:S(2)}) copy-start(bf16[32,1024]{1,0:T(8,128)(2,1)} %param.12) | copy-start | bytes 196612
  5.3 13.1 %copy-start.9 = (bf16[32,1024]{1,0:T(8,128)(2,1)S(1)}, bf16[32,1024]{1,0:T(8,128)(2,1)}, u32[]{:S(2)}) copy-start(bf16[32,1024]{1,0:T(8,128)(2,1)} %param.11) | copy-start | bytes 196612
  5.3 13.2 %copy-start.7 = (bf16[32,8192]{1,0:T(8,128)(2,1)S(1)}, bf16[32,8192]{1,0:T(8,128)(2,1)}, u32[]{:S(2)}) copy-start(bf16[32,8192]{1,0:T(8,128)(2,1)} %param.10) | copy-start | bytes 1572868
  5.3 19.4 %copy-start.6 = (s32[8192]{0:T(1024)S(1)}, s32[8192]{0:T(1024)}, u32[]{:S(2)}) copy-start(s32[8192]{0:T(1024)} %param.16) | copy-start | bytes 98308
  5.3 87.2 %all-to-all-start = ((bf16[32,24,16,128]{3,2,1,0:T(8,128)(2,1)}), bf16[32,24,16,128]{3,2,1,0:T(8,128)(2,1)}, u32[]{:S(2)}, u32[]{:S(2)}) async-start(bf16[32,24,16,128]{3,2,1,0:T(8,128)(2,1)} %pack_blocks.1), calls=%async_computation | async-start | bytes 6291456 | tf_op jit(solution)/shard_map/all_to_all | solution.py:335
  18.2 9.0 %copy-start.11 = (s32[32]{0:T(128)S(1)}, s32[32]{0:T(128)}, u32[]{:S(2)}) copy-start(s32[32]{0:T(128)} %param.19) | copy-start | bytes 388
  18.3 9.6 %copy-start.10 = (s32[32,16]{0,1:T(8,128)S(1)}, s32[32,16]{0,1:T(8,128)}, u32[]{:S(2)}) copy-start(s32[32,16]{0,1:T(8,128)} %param.18) | copy-start | bytes 6148
  18.5 9.4 %collective-permute-start = (bf16[32,1280]{1,0:T(8,128)(2,1)S(1)}, bf16[32,1280]{1,0:T(8,128)(2,1)S(1)}, u32[]{:S(2)}, u32[]{:S(2)}) collective-permute-start(bf16[32,1280]{1,0:T(8,128)(2,1)S(1)} %pad_maximum_fusion.1), channel_id=1, source_target_pairs={{0,1},{1,0},{2,3},{3,2},{4,5},{5,4},{6,7},{7,6},{8,9},{9,8},{10,11... | collective-permute-start | bytes 245768 | tf_op jit(solution)/shard_map/ppermute | solution.py:349
  19.8 11.9 %collective-permute-start.1 = (bf16[32,1280]{1,0:T(8,128)(2,1)S(1)}, bf16[32,1280]{1,0:T(8,128)(2,1)S(1)}, u32[]{:S(2)}, u32[]{:S(2)}) collective-permute-start(bf16[32,1280]{1,0:T(8,128)(2,1)S(1)} %pad_maximum_fusion.2), channel_id=1, source_target_pairs={{0,2},{1,3},{2,0},{3,1},{4,6},{5,7},{6,4},{7,5},{8,10},{9,11},{10,... | collective-permute-start | bytes 245768 | tf_op jit(solution)/shard_map/ppermute | solution.py:349
  22.4 11.1 %collective-permute-start.2 = (bf16[32,1280]{1,0:T(8,128)(2,1)S(1)}, bf16[32,1280]{1,0:T(8,128)(2,1)S(1)}, u32[]{:S(2)}, u32[]{:S(2)}) collective-permute-start(bf16[32,1280]{1,0:T(8,128)(2,1)S(1)} %pad_maximum_fusion.3), channel_id=1, source_target_pairs={{0,3},{1,2},{2,1},{3,0},{4,7},{5,6},{6,5},{7,4},{8,11},{9,10},{10,... | collective-permute-start | bytes 245768 | tf_op jit(solution)/shard_map/ppermute | solution.py:349
  22.7 10.8 %collective-permute-start.3 = (bf16[32,1280]{1,0:T(8,128)(2,1)S(1)}, bf16[32,1280]{1,0:T(8,128)(2,1)S(1)}, u32[]{:S(2)}, u32[]{:S(2)}) collective-permute-start(bf16[32,1280]{1,0:T(8,128)(2,1)S(1)} %pad_maximum_fusion.4), channel_id=1, source_target_pairs={{0,4},{1,5},{2,6},{3,7},{4,0},{5,1},{6,2},{7,3},{8,12},{9,13},{10,... | collective-permute-start | bytes 245768 | tf_op jit(solution)/shard_map/ppermute | solution.py:349
  23.1 10.3 %collective-permute-start.4 = (bf16[32,1280]{1,0:T(8,128)(2,1)S(1)}, bf16[32,1280]{1,0:T(8,128)(2,1)S(1)}, u32[]{:S(2)}, u32[]{:S(2)}) collective-permute-start(bf16[32,1280]{1,0:T(8,128)(2,1)S(1)} %pad_maximum_fusion.5), channel_id=1, source_target_pairs={{0,5},{1,4},{2,7},{3,6},{4,1},{5,0},{6,3},{7,2},{8,13},{9,12},{10,... | collective-permute-start | bytes 245768 | tf_op jit(solution)/shard_map/ppermute | solution.py:349
  27.9 6.2 %collective-permute-start.5 = (bf16[32,1280]{1,0:T(8,128)(2,1)S(1)}, bf16[32,1280]{1,0:T(8,128)(2,1)S(1)}, u32[]{:S(2)}, u32[]{:S(2)}) collective-permute-start(bf16[32,1280]{1,0:T(8,128)(2,1)S(1)} %pad_maximum_fusion.6), channel_id=1, source_target_pairs={{0,6},{1,7},{2,4},{3,5},{4,2},{5,3},{6,0},{7,1},{8,14},{9,15},{10,... | collective-permute-start | bytes 245768 | tf_op jit(solution)/shard_map/ppermute | solution.py:349
  31.7 6.5 %collective-permute-start.6 = (bf16[32,1280]{1,0:T(8,128)(2,1)S(1)}, bf16[32,1280]{1,0:T(8,128)(2,1)S(1)}, u32[]{:S(2)}, u32[]{:S(2)}) collective-permute-start(bf16[32,1280]{1,0:T(8,128)(2,1)S(1)} %pad_maximum_fusion.7), channel_id=1, source_target_pairs={{0,7},{1,6},{2,5},{3,4},{4,3},{5,2},{6,1},{7,0},{8,15},{9,14},{10,... | collective-permute-start | bytes 245768 | tf_op jit(solution)/shard_map/ppermute | solution.py:349
  33.4 65.2 %copy-start.2 = (s32[3]{0:T(128)}, s32[3]{0:T(128)S(1)}, u32[]{:S(2)}) copy-start(s32[3]{0:T(128)S(1)} %pad_add_fusion.info) | copy-start | bytes 40
  42.8 1.4 copy-start.3
  44.2 1.0 copy-start.4
  45.1 0.8 copy-start.5
  92.4 95.4 %all-to-all-start.1 = ((bf16[32,2,16,128]{3,2,1,0:T(8,128)(2,1)}), bf16[32,2,16,128]{3,2,1,0:T(8,128)(2,1)S(1)}, u32[]{:S(2)}, u32[]{:S(2)}) async-start(bf16[32,2,16,128]{3,2,1,0:T(8,128)(2,1)} %get-tuple-element.26), calls=%async_computation.1 | async-start | bytes 524288 | tf_op jit(solution)/shard_map/all_to_all | solution.py:365
  98.6 93.1 %copy-start = (bf16[256,16,128]{2,1,0:T(8,128)(2,1)S(1)}, bf16[256,16,128]{2,1,0:T(8,128)(2,1)}, u32[]{:S(2)}) copy-start(bf16[256,16,128]{2,1,0:T(8,128)(2,1)} %keys.1) | copy-start | bytes 3145732
  98.6 93.1 %copy-start.1 = (bf16[256,16,128]{2,1,0:T(8,128)(2,1)S(1)}, bf16[256,16,128]{2,1,0:T(8,128)(2,1)}, u32[]{:S(2)}) copy-start(bf16[256,16,128]{2,1,0:T(8,128)(2,1)} %values.1) | copy-start | bytes 3145732
  187.9 14.0 %all-to-all-start.2 = ((bf16[8,32,1024]{2,1,0:T(8,128)(2,1)}), bf16[8,32,1024]{2,1,0:T(8,128)(2,1)S(1)}, u32[]{:S(2)}, u32[]{:S(2)}) async-start(bf16[8,32,1024]{2,1,0:T(8,128)(2,1)} %bitcast.16), calls=%async_computation.2 | async-start | bytes 1048576 | tf_op jit(solution)/shard_map/all_to_all | solution.py:369

commit v3 on v2

--- a/solution.py
+++ b/solution.py
@@ -11,6 +11,8 @@
 GROUP = H // KVH
 BLK = 16
 POOL = 32
+LANES = 4
+LEVELS = POOL // LANES
 TENSOR = 8
 SLOTS = 256
 PBLK = 256
@@ -19,7 +21,7 @@
 NEWB = TOK // BLK
 LOAD = 2 * CAP
 PART = 8
-WIDE = 60 * 1024 * 1024
+WIDE = 57 * 1024 * 1024
 SCALE = HD ** (-0.5) * 1.4426950408889634
 neg_big = -1e30
 
@@ -31,6 +33,10 @@
 SMEM = pl.BlockSpec(memory_space=pltpu.SMEM)
 HBM = pl.BlockSpec(memory_space=pltpu.HBM)
 NT = (((1,), (1,)), ((), ()))
+
+
+def with_ones(values):
+    return jnp.concatenate([values, jnp.ones(values.shape, bf16)], axis=1)
 
 
 def cost(flops, moved, exps=0):
@@ -136,14 +142,15 @@
 
 def gather_kernel(info, evict, *refs):
     pieces = refs[:TENSOR]
-    heads, shift, start, sends, own_keys, own_values = refs[TENSOR:]
+    heads, start, sends, own_keys, own_values = refs[TENSOR:]
     t, count, me = info[0], info[1], info[2]
+    lane = me & (LANES - 1)
     rows = TOK // TENSOR
     for k in range(TENSOR):
         begin = pl.multiple_of((t ^ k) * rows, rows)
         at = pl.ds(begin, rows)
         for h in range(GROUP):
-            heads[pl.ds(pl.multiple_of(h * TOK + begin, rows), rows), :] = pieces[k][
+            heads[pl.ds(pl.multiple_of(h * TOK + begin, rows), rows), :HD] = pieces[k][
                 :, h * HD : (h + 1) * HD
             ]
         own_keys[at, :] = pieces[k][:, GROUP * HD : (GROUP + 1) * HD]
@@ -154,19 +161,19 @@
         live = j * BLK + place < count
         for part, own in enumerate((own_keys, own_values)):
             block = own[j * BLK : (j + 1) * BLK, :]
-            sends[owner, part] = jnp.where(live, block.astype(f32), 0.0).astype(bf16)
-    both = jnp.concatenate([own_values[...], jnp.ones((TOK, HD), bf16)], axis=1)
+            sends[(owner & (LANES - 1)) ^ lane, owner // LANES, part] = jnp.where(live, block.astype(f32), 0.0).astype(bf16)
+    both = with_ones(own_values[...])
     row = lax.broadcasted_iota(i32, (TOK, TOK), 0)
     column = lax.broadcasted_iota(i32, (TOK, TOK), 1)
 
     @pl.loop(0, GROUP)
     def _(h):
         at = pl.ds(pl.multiple_of(h * TOK, TOK), TOK)
-        scores = lax.dot_general(heads[at, :], own_keys[...], NT, preferred_element_type=f32)
+        scores = lax.dot_general(heads[at, :HD], own_keys[...], NT, preferred_element_type=f32)
         scores = jnp.where(column <= row, scores * SCALE, neg_big)
-        top = jnp.max(scores, axis=1, keepdims=True)
-        shift[at, :] = jnp.broadcast_to(top, (TOK, HD))
-        weights = jnp.exp2(scores - top).astype(bf16)
+        top = jnp.max(scores, axis=1, keepdims=True).astype(bf16)
+        heads[at, HD:] = jnp.broadcast_to(top, (TOK, HD))
+        weights = jnp.exp2(scores - top.astype(f32)).astype(bf16)
         start[at, :] = jnp.dot(weights, both, preferred_element_type=f32)
 
 
@@ -174,13 +181,12 @@
     return pl.pallas_call(
         gather_kernel,
         out_shape=[
-            jax.ShapeDtypeStruct((GROUP * TOK, HD), bf16),
-            jax.ShapeDtypeStruct((GROUP * TOK, HD), f32),
+            jax.ShapeDtypeStruct((GROUP * TOK, 2 * HD), bf16),
             jax.ShapeDtypeStruct((GROUP * TOK, 2 * HD), f32),
-            jax.ShapeDtypeStruct((POOL, 2, BLK, HD), bf16),
+            jax.ShapeDtypeStruct((LANES, LEVELS, 2, BLK, HD), bf16),
         ],
         in_specs=[SMEM, SMEM] + [VMEM] * TENSOR,
-        out_specs=[VMEM] * 4,
+        out_specs=[VMEM] * 3,
         scratch_shapes=[pltpu.VMEM((TOK, HD), bf16), pltpu.VMEM((TOK, HD), bf16)],
         compiler_params=pltpu.CompilerParams(vmem_limit_bytes=16 * 1024 * 1024),
         cost_estimate=cost(10**9, 4 * 10**6),
@@ -188,64 +194,83 @@
     )(info, evict_slots, *pieces)
 
 
-def write_kernel(target, keys, values, arrived, out_keys, out_values):
+def write_kernel(info, target, keys, values, arrived, out_keys, out_values):
+    lane = info[2] & (LANES - 1)
     out_keys[...] = keys[...]
     out_values[...] = values[...]
-    for g in range(POOL):
-        slot = target[g]
-
-        @pl.when(slot >= 0)
-        def _():
-            out_keys[slot] = arrived[g, 0]
-            out_values[slot] = arrived[g, 1]
-
-
-def write(target, pool_keys, pool_values, arrived):
+    for level in range(LEVELS):
+        for m in range(LANES):
+            slot = target[level * LANES + (lane ^ m)]
+
+            @pl.when(slot >= 0)
+            def _():
+                out_keys[slot] = arrived[level, m, 0]
+                out_values[slot] = arrived[level, m, 1]
+
+
+def write(info, target, pool_keys, pool_values, arrived):
     return pl.pallas_call(
         write_kernel,
         out_shape=[jax.ShapeDtypeStruct(pool_keys.shape, bf16)] * 2,
-        in_specs=[SMEM] + [VMEM] * 3,
+        in_specs=[SMEM, SMEM] + [VMEM] * 3,
         out_specs=[VMEM] * 2,
         compiler_params=pltpu.CompilerParams(vmem_limit_bytes=16 * 1024 * 1024),
         cost_estimate=cost(10**6, 4 * 10**6),
         name="write_blocks",
-    )(target, pool_keys, pool_values, arrived)
+    )(info, target, pool_keys, pool_values, arrived)
 
 
 KEYS = PBLK * BLK
 ROWS = 1024
 TILE = 256
 SMALL = 256
-
-
-def attend_kernel(
-    info, where_from, heads_h, shift_h, start_h, got, out, keys, values, heads, shift, start, sems
-):
-    copies = [
-        pltpu.make_async_copy(source, target, sems.at[i])
-        for i, (source, target) in enumerate(
-            [(heads_h, heads), (shift_h, shift), (start_h, start)]
-        )
-    ]
-    for copy in copies:
+SPLIT = 8
+
+
+def attend_kernel(info, where_from, heads_h, start_h, got_h, out_h, *scratch):
+    got, keys, values, heads, start, out, sems, got_sems, out_sems = scratch
+    blocks = GROUP * TOK // ROWS
+    part = got.shape[0] // SPLIT
+    coming = []
+    for i in range(SPLIT):
+        at = pl.ds(i * part, part)
+        coming.append(pltpu.make_async_copy(got_h.at[at], got.at[at], got_sems.at[i]))
+    head_copies, start_copies = [], []
+    for i in range(blocks):
+        rows = pl.ds(i * ROWS, ROWS)
+        head_copies.append(
+            pltpu.make_async_copy(heads_h.at[rows], heads.at[rows], sems.at[i, 0])
+        )
+        start_copies.append(
+            pltpu.make_async_copy(start_h.at[rows], start.at[rows], sems.at[i, 1])
+        )
+    for copy in coming + head_copies[:1]:
+        copy.start()
+    for copy in coming:
+        copy.wait()
+    for copy in head_copies[1:] + start_copies:
         copy.start()
     for b in range(PBLK):
         index = where_from[b]
         keys[b * BLK : (b + 1) * BLK, :] = got[index]
         values[b * BLK : (b + 1) * BLK, :] = got[index + CAP]
-    for copy in copies:
-        copy.wait()
-    ones = jnp.ones((TILE, HD), bf16)
     live = lax.broadcasted_iota(i32, (TOK, HD), 0) < info[1]
+    leaving = [
+        pltpu.make_async_copy(
+            out.at[:, pl.ds(h * HD, HD)], out_h.at[:, pl.ds(h * HD, HD)], out_sems.at[h]
+        )
+        for h in range(GROUP)
+    ]
 
     def finish(h, summed):
         result = summed[:, :HD] / summed[:, HD:]
         out[:, h * HD : (h + 1) * HD] = jnp.where(live, result, 0.0).astype(bf16)
 
-    for i in range(GROUP * TOK // ROWS):
-        query = heads[i * ROWS : (i + 1) * ROWS, :]
-        top = shift[i * ROWS : (i + 1) * ROWS, :]
-        summed = start[i * ROWS : (i + 1) * ROWS, :]
+    for i in range(blocks):
+        head_copies[i].wait()
+        query = heads[i * ROWS : (i + 1) * ROWS, :HD]
+        top = heads[i * ROWS : (i + 1) * ROWS, HD:].astype(f32)
+        summed = None
         for j in range(KEYS // TILE):
             tile = slice(j * TILE, (j + 1) * TILE)
             part = lax.dot_general(query, keys[tile, :], NT, preferred_element_type=f32)
@@ -256,8 +281,10 @@
                 ],
                 axis=1,
             ).astype(bf16)
-            both = jnp.concatenate([values[tile, :], ones], axis=1)
-            summed = summed + jnp.dot(weights, both, preferred_element_type=f32)
+            more = jnp.dot(weights, with_ones(values[tile, :]), preferred_element_type=f32)
+            summed = more if summed is None else summed + more
+        start_copies[i].wait()
+        summed = summed + start[i * ROWS : (i + 1) * ROWS, :]
         for h in range(ROWS // TOK):
             finish(i * (ROWS // TOK) + h, summed[h * TOK : (h + 1) * TOK, :])
         largest = jnp.max(summed[:, HD:])
@@ -272,43 +299,53 @@
                     tile = pl.ds(pl.multiple_of(j * SMALL, SMALL), SMALL)
                     part = (
                         lax.dot_general(
-                            heads[at, :], keys[tile, :], NT, preferred_element_type=f32
+                            heads[at, :HD], keys[tile, :], NT, preferred_element_type=f32
                         )
                         * SCALE
                     )
                     above = jnp.maximum(best, jnp.max(part, axis=1, keepdims=True))
                     weights = jnp.exp2(part - above).astype(bf16)
-                    both = jnp.concatenate([values[tile, :], ones], axis=1)
                     summed = summed * jnp.exp2(best - above) + jnp.dot(
-                        weights, both, preferred_element_type=f32
+                        weights, with_ones(values[tile, :]), preferred_element_type=f32
                     )
                     return above, summed
 
                 best, summed = lax.fori_loop(
-                    0, KEYS // SMALL, one, (shift[at, :1], start[at, :])
+                    0,
+                    KEYS // SMALL,
+                    one,
+                    (heads[at, HD : HD + 1].astype(f32), start[at, :]),
                 )
                 finish(i * (ROWS // TOK) + h, summed)
 
-
-def attend(info, where_from, heads, shift, start, got):
+        for h in range(i * (ROWS // TOK), (i + 1) * (ROWS // TOK)):
+            leaving[h].start()
+    for copy in leaving:
+        copy.wait()
+
+
+def attend(info, where_from, heads, start, got):
     blocks = got.shape[0] * got.shape[1]
     return pl.pallas_call(
         attend_kernel,
         out_shape=jax.ShapeDtypeStruct((TOK, GROUP * HD), bf16),
-        in_specs=[SMEM, SMEM] + [HBM] * 3 + [VMEM],
-        out_specs=VMEM,
+        in_specs=[SMEM, SMEM, HBM, HBM, HBM],
+        out_specs=HBM,
         scratch_shapes=[
+            pltpu.VMEM((blocks, BLK, HD), bf16),
             pltpu.VMEM((KEYS, HD), bf16),
             pltpu.VMEM((KEYS, HD), bf16),
             pltpu.VMEM(heads.shape, bf16),
-            pltpu.VMEM(shift.shape, f32),
             pltpu.VMEM(start.shape, f32),
-            pltpu.SemaphoreType.DMA((3,)),
+            pltpu.VMEM((TOK, GROUP * HD), bf16),
+            pltpu.SemaphoreType.DMA((GROUP * TOK // ROWS, 2)),
+            pltpu.SemaphoreType.DMA((SPLIT,)),
+            pltpu.SemaphoreType.DMA((GROUP,)),
         ],
-        compiler_params=pltpu.CompilerParams(vmem_limit_bytes=57 * 1024 * 1024),
+        compiler_params=pltpu.CompilerParams(vmem_limit_bytes=WIDE),
         cost_estimate=cost(9 * 10**9, 6 * 10**6, 9 * 10**6),
         name="attend",
-    )(info, where_from, heads, shift, start, got.reshape(blocks, BLK, HD))
+    )(info, where_from, heads, start, got.reshape(blocks, BLK, HD))
 
 
 def local(
@@ -360,15 +397,23 @@
 
     target = jnp.max(jnp.where(evict_slots // SLOTS == me, evict_slots % SLOTS, -1), axis=1)
 
-    heads, shift, start, sends = gather(info, evict_slots, pieces)
+    heads, start, sends = gather(info, evict_slots, pieces)
+    turned = [sends[0]] + [
+        lax.ppermute(sends[m], "pool", [(s, s ^ m) for s in range(POOL)])
+        for m in range(1, LANES)
+    ]
+    sends = jnp.stack(turned, axis=1)
     got, sends = lax.optimization_barrier((got, sends))
-    arrived = lax.all_to_all(sends, "pool", split_axis=0, concat_axis=0, tiled=True)
-    result = attend(info, where_from, heads, shift, start, got)
+    columns = [[level * LANES + lane for level in range(LEVELS)] for lane in range(LANES)]
+    arrived = lax.all_to_all(
+        sends, "pool", split_axis=0, concat_axis=0, tiled=True, axis_index_groups=columns
+    )
+    result = attend(info, where_from, heads, start, got)
     result, arrived = lax.optimization_barrier((result, arrived))
     result = result.reshape(TENSOR, share, GROUP * HD)
     attended = lax.all_to_all(result, "tensor", split_axis=0, concat_axis=0, tiled=True)
     attended = jnp.transpose(attended, (1, 0, 2)).reshape(share, H * HD)
-    new_pool_keys, new_pool_values = write(target, pool_keys, pool_values, arrived)
+    new_pool_keys, new_pool_values = write(info, target, pool_keys, pool_values, arrived)
     return (attended, new_pool_keys, new_pool_values)
 
 

time: 203 us -> 200 us (0.985)
  waiting for transfers between devices: 59.2 us -> 49.8 us
  starting transfers between devices: 33.1 us -> 39.7 us
    all_to_all x1, waiting for transfers between devices: 46.5 us -> 35.2 us  [local(): got = lax.all_to_all(send, 'pool', split_axis=0, concat_axis=0, tiled=True)]
    ppermute x0 -> x3, starting transfers between devices: none -> 8.32 us  [local(): lax.ppermute(sends[m], 'pool', [(s, s ^ m) for s in range(POOL)])]
    ppermute x0 -> x3, waiting for transfers between devices: none -> 3.02 us  [local(): lax.ppermute(sends[m], 'pool', [(s, s ^ m) for s in range(POOL)])]
    all_to_all x1, starting transfers between devices: 6.15 us -> 3.59 us  [local(): lax.all_to_all(sends, 'pool', split_axis=0, concat_axis=0, tiled=True, ax...]
  transfers between devices with their start and end apart: 10 -> 13, of which waited for: 4 -> 5; matrix products, arithmetic and copies ran while one was open for 2% -> 3% of each run, Pallas kernels for 47% -> 48%
where the time goes in v3:
time: 200 us
  Pallas kernels  100 us (50%)
  waiting for transfers between devices  49.8 us (25%)
  starting transfers between devices  39.7 us (20%)
  local copies, waits for them, and re-layouts  6.3 us (3%)
  other arithmetic  3.05 us (2%)
    pallas_call x1, Pallas kernels, attend(): pl.pallas_call(attend_kernel, out_shape=jax.ShapeDtypeStruct((TOK, GROUP...  88.9 us
    all_to_all x1, waiting for transfers between devices, local(): got = lax.all_to_all(send, 'pool', split_axis=0, concat_axis=0, tiled=True)  35.2 us
    all_to_all x1, starting transfers between devices, local(): got = lax.all_to_all(send, 'pool', split_axis=0, concat_axis=0, tiled=True)  12.9 us
    ppermute x7, starting transfers between devices, local(): piece = lax.ppermute(piece, 'tensor', [(s, s ^ k) for s in range(TENSOR)])  10.3 us
    ppermute x3, starting transfers between devices, local(): lax.ppermute(sends[m], 'pool', [(s, s ^ m) for s in range(POOL)])  8.32 us
    all_to_all x1, waiting for transfers between devices, local(): lax.all_to_all(result, 'tensor', split_axis=0, concat_axis=0, tiled=True)  6.7 us
    ppermute x7, waiting for transfers between devices, local(): piece = lax.ppermute(piece, 'tensor', [(s, s ^ k) for s in range(TENSOR)])  4.88 us
    pallas_call x1, Pallas kernels, pack(): pl.pallas_call(pack_kernel, out_shape=jax.ShapeDtypeStruct((POOL, LOAD, B...  4.6 us
  transfers between devices with their start and end apart: 13, of which 5 were waited for; matrix products, arithmetic and copies ran while one was open for 3% of the time, Pallas kernels for 48%

profile of v3, /device:TPU:1, one launch (start us, length us, event | category | flops | bytes accessed | tf_op | source)
XLA Modules:
  0.0 200.0 jit_solution(1495545456423231365)
XLA Ops:
  0.6 4.6 %pack_blocks.1 = bf16[32,24,16,128]{3,2,1,0:T(8,128)(2,1)} custom-call(s32[1]{0:T(128)} %bitcast.1.me, s32[32,256]{1,0:T(8,128)} %prefix_h.1, s32[64,128]{1,0:T(8,128)} %bitcast.25, s32[64,128]{1,0:T(8,128)} %bitcast.32, bf16[256,16,128]{2,1,0:T(8,128)(2,1)} %keys.1, bf16[256,16,128]{2,1,0:T(8,128)(2,1)} %values.1), custom_call_target="tpu_custom_call" | custom-call | flops 1000000000 | bytes 5000000 | tf_op jit(solution)/shard_map/pack_blocks/pallas_call | solution.py:112
  5.3 12.9 %all-to-all-start = ((bf16[32,24,16,128]{3,2,1,0:T(8,128)(2,1)}), bf16[32,24,16,128]{3,2,1,0:T(8,128)(2,1)}, u32[]{:S(2)}, u32[]{:S(2)}) async-start(bf16[32,24,16,128]{3,2,1,0:T(8,128)(2,1)} %pack_blocks.1), calls=%async_computation | async-start | bytes 6291456 | tf_op jit(solution)/shard_map/all_to_all | solution.py:372
  18.5 1.3 collective-permute-start
  19.8 2.5 %collective-permute-start.1 = (bf16[32,1280]{1,0:T(8,128)(2,1)S(1)}, bf16[32,1280]{1,0:T(8,128)(2,1)S(1)}, u32[]{:S(2)}, u32[]{:S(2)}) collective-permute-start(bf16[32,1280]{1,0:T(8,128)(2,1)S(1)} %pad_maximum_fusion.3), channel_id=1, source_target_pairs={{0,2},{1,3},{2,0},{3,1},{4,6},{5,7},{6,4},{7,5},{8,10},{9,11},{10,... | collective-permute-start | bytes 245768 | tf_op jit(solution)/shard_map/ppermute | solution.py:386
  23.2 0.9 collective-permute-start.4
  25.3 1.7 gather_fusion
  27.4 3.9 %collective-permute-start.5 = (bf16[32,1280]{1,0:T(8,128)(2,1)S(1)}, bf16[32,1280]{1,0:T(8,128)(2,1)S(1)}, u32[]{:S(2)}, u32[]{:S(2)}) collective-permute-start(bf16[32,1280]{1,0:T(8,128)(2,1)S(1)} %pad_maximum_fusion.7), channel_id=1, source_target_pairs={{0,6},{1,7},{2,4},{3,5},{4,2},{5,3},{6,0},{7,1},{8,14},{9,15},{10,... | collective-permute-start | bytes 245768 | tf_op jit(solution)/shard_map/ppermute | solution.py:386
  31.3 1.0 collective-permute-start.6
  33.0 0.9 collective-permute-done.5.refs_6_
  33.9 4.0 %collective-permute-done.6.refs_7_ = bf16[32,1280]{1,0:T(8,128)(2,1)S(1)} collective-permute-done((bf16[32,1280]{1,0:T(8,128)(2,1)S(1)}, bf16[32,1280]{1,0:T(8,128)(2,1)S(1)}, u32[]{:S(2)}, u32[]{:S(2)}) %collective-permute-start.6) | collective-permute-done | bytes 81952 | tf_op jit(solution)/shard_map/ppermute | solution.py:386
  37.9 4.4 %gather_rows.1 = (bf16[2048,256]{1,0:T(8,128)(2,1)S(1)}, f32[2048,256]{1,0:T(8,128)S(1)}, bf16[4,8,2,16,128]{4,3,2,1,0:T(8,128)(2,1)S(1)}) custom-call(s32[3]{0:T(128)S(1)} %pad_add_fusion.info, s32[32,16]{1,0:T(8,128)S(1)} %copy.17.evict, bf16[32,1280]{1,0:T(8,128)(2,1)S(1)} %pad_maximum_fusion.1.refs_0_, ...), custom_call_target="tpu_custom_call" | custom-call | flops 1000000000 | bytes 4000000 | tf_op jit(solution)/shard_map/gather_rows/pallas_call | solution.py:181
  42.3 1.3 copy-done.4
  43.6 1.0 copy-done.5
  44.6 6.3 %collective-permute-start.9 = (bf16[8,2,16,128]{3,2,1,0:T(8,128)(2,1)S(1)}, bf16[8,2,16,128]{3,2,1,0:T(8,128)(2,1)S(1)}, u32[]{:S(2)}, u32[]{:S(2)}) collective-permute-start(bf16[8,2,16,128]{3,2,1,0:T(8,128)(2,1)S(1)} %get-tuple-element.40), channel_id=1, source_target_pairs={{0,24},{8,16},{16,8},{24,0},{32,56},{40,48},{48,40},{56,32},{64,88... | collective-permute-start | bytes 196616 | tf_op jit(solution)/shard_map/ppermute | solution.py:402
  51.0 2.0 collective-permute-start.8
  53.5 3.0 %collective-permute-done.8 = bf16[8,2,16,128]{3,2,1,0:T(8,128)(2,1)S(1)} collective-permute-done((bf16[8,2,16,128]{3,2,1,0:T(8,128)(2,1)S(1)}, bf16[8,2,16,128]{3,2,1,0:T(8,128)(2,1)S(1)}, u32[]{:S(2)}, u32[]{:S(2)}) %collective-permute-start.8) | collective-permute-done | bytes 65568 | tf_op jit(solution)/shard_map/ppermute | solution.py:402
  56.6 0.7 pad_maximum_fusion
  57.3 35.2 %all-to-all-done = bf16[32,24,16,128]{3,2,1,0:T(8,128)(2,1)} async-done(((bf16[32,24,16,128]{3,2,1,0:T(8,128)(2,1)}), bf16[32,24,16,128]{3,2,1,0:T(8,128)(2,1)}, u32[]{:S(2)}, u32[]{:S(2)}) %all-to-all-start) | async-done | bytes 3145760 | tf_op jit(solution)/shard_map/all_to_all | solution.py:372
  92.5 3.6 %all-to-all-start.1 = ((bf16[8,4,2,16,128]{4,3,2,1,0:T(8,128)(2,1)}), bf16[8,4,2,16,128]{4,3,2,1,0:T(8,128)(2,1)S(1)}, u32[]{:S(2)}, u32[]{:S(2)}) async-start(bf16[8,4,2,16,128]{4,3,2,1,0:T(8,128)(2,1)} %pad_maximum_fusion), calls=%async_computation.1 | async-start | bytes 524288 | tf_op jit(solution)/shard_map/all_to_all | solution.py:408
  96.1 88.9 %attend.1 = bf16[256,1024]{1,0:T(8,128)(2,1)} custom-call(s32[3]{0:T(128)} %copy-done.2, s32[256]{0:T(256)} %add_subtract_fusion.where_from, bf16[2048,256]{1,0:T(8,128)(2,1)} %copy-done.5, f32[2048,256]{1,0:T(8,128)} %copy-done.4, bf16[768,16,128]{2,1,0:T(8,128)(2,1)} %bitcast.13.got_h), custom_call_target="tpu_custom_call" | custom-call | flops 8999999488 | bytes 6000000 | tf_op jit(solution)/shard_map/attend/pallas_call | solution.py:329
  185.0 4.5 %all-to-all-start.2 = ((bf16[8,32,1024]{2,1,0:T(8,128)(2,1)}), bf16[8,32,1024]{2,1,0:T(8,128)(2,1)S(1)}, u32[]{:S(2)}, u32[]{:S(2)}) async-start(bf16[8,32,1024]{2,1,0:T(8,128)(2,1)} %bitcast.27), calls=%async_computation.2 | async-start | bytes 1048576 | tf_op jit(solution)/shard_map/all_to_all | solution.py:414
  190.2 2.2 %write_blocks.1 = (bf16[256,16,128]{2,1,0:T(8,128)(2,1)}, bf16[256,16,128]{2,1,0:T(8,128)(2,1)}) custom-call(s32[3]{0:T(128)S(1)} %copy-done.3, s32[32]{0:T(128)S(1)} %fusion.2.target, bf16[256,16,128]{2,1,0:T(8,128)(2,1)S(1)} %copy-done, bf16[256,16,128]{2,1,0:T(8,128)(2,1)S(1)} %copy-done.1, bf16[8,4,2,16,128]{4,3,2,1,0:T(8,128)(2,1)S(1)} %all-to-all-done.1.arrived), custom_call_target="tpu_custom_call" | custom-call | flops 1000000 | bytes 4000000 | tf_op jit(solution)/shard_map/write_blocks/pallas_call | solution.py:212
  192.4 6.7 %all-to-all-done.2 = bf16[8,32,1024]{2,1,0:T(8,128)(2,1)S(1)} async-done(((bf16[8,32,1024]{2,1,0:T(8,128)(2,1)}), bf16[8,32,1024]{2,1,0:T(8,128)(2,1)S(1)}, u32[]{:S(2)}, u32[]{:S(2)}) %all-to-all-start.2) | async-done | bytes 524320 | tf_op jit(solution)/shard_map/all_to_all | solution.py:414
  199.1 0.8 copy.19
  (53 shorter events, 4.5 us)
Async XLA Ops:
  5.2 13.1 %copy-start.8 = (bf16[32,1024]{1,0:T(8,128)(2,1)S(1)}, bf16[32,1024]{1,0:T(8,128)(2,1)}, u32[]{:S(2)}) copy-start(bf16[32,1024]{1,0:T(8,128)(2,1)} %param.12) | copy-start | bytes 196612
  5.3 13.1 %copy-start.9 = (bf16[32,1024]{1,0:T(8,128)(2,1)S(1)}, bf16[32,1024]{1,0:T(8,128)(2,1)}, u32[]{:S(2)}) copy-start(bf16[32,1024]{1,0:T(8,128)(2,1)} %param.11) | copy-start | bytes 196612
  5.3 13.2 %copy-start.7 = (bf16[32,8192]{1,0:T(8,128)(2,1)S(1)}, bf16[32,8192]{1,0:T(8,128)(2,1)}, u32[]{:S(2)}) copy-start(bf16[32,8192]{1,0:T(8,128)(2,1)} %param.10) | copy-start | bytes 1572868
  5.3 18.7 %copy-start.11 = (s32[32]{0:T(128)S(1)}, s32[32]{0:T(128)}, u32[]{:S(2)}) copy-start(s32[32]{0:T(128)} %param.19) | copy-start | bytes 388
  5.3 20.0 %copy-start.6 = (s32[8192]{0:T(1024)S(1)}, s32[8192]{0:T(1024)}, u32[]{:S(2)}) copy-start(s32[8192]{0:T(1024)} %param.16) | copy-start | bytes 98308
  5.3 87.2 %all-to-all-start = ((bf16[32,24,16,128]{3,2,1,0:T(8,128)(2,1)}), bf16[32,24,16,128]{3,2,1,0:T(8,128)(2,1)}, u32[]{:S(2)}, u32[]{:S(2)}) async-start(bf16[32,24,16,128]{3,2,1,0:T(8,128)(2,1)} %pack_blocks.1), calls=%async_computation | async-start | bytes 6291456 | tf_op jit(solution)/shard_map/all_to_all | solution.py:372
  18.3 8.8 %copy-start.10 = (s32[32,16]{0,1:T(8,128)S(1)}, s32[32,16]{0,1:T(8,128)}, u32[]{:S(2)}) copy-start(s32[32,16]{0,1:T(8,128)} %param.18) | copy-start | bytes 6148
  18.5 8.9 %collective-permute-start = (bf16[32,1280]{1,0:T(8,128)(2,1)S(1)}, bf16[32,1280]{1,0:T(8,128)(2,1)S(1)}, u32[]{:S(2)}, u32[]{:S(2)}) collective-permute-start(bf16[32,1280]{1,0:T(8,128)(2,1)S(1)} %pad_maximum_fusion.2), channel_id=1, source_target_pairs={{0,1},{1,0},{2,3},{3,2},{4,5},{5,4},{6,7},{7,6},{8,9},{9,8},{10,11... | collective-permute-start | bytes 245768 | tf_op jit(solution)/shard_map/ppermute | solution.py:386
  19.8 11.4 %collective-permute-start.1 = (bf16[32,1280]{1,0:T(8,128)(2,1)S(1)}, bf16[32,1280]{1,0:T(8,128)(2,1)S(1)}, u32[]{:S(2)}, u32[]{:S(2)}) collective-permute-start(bf16[32,1280]{1,0:T(8,128)(2,1)S(1)} %pad_maximum_fusion.3), channel_id=1, source_target_pairs={{0,2},{1,3},{2,0},{3,1},{4,6},{5,7},{6,4},{7,5},{8,10},{9,11},{10,... | collective-permute-start | bytes 245768 | tf_op jit(solution)/shard_map/ppermute | solution.py:386
  22.4 10.6 %collective-permute-start.2 = (bf16[32,1280]{1,0:T(8,128)(2,1)S(1)}, bf16[32,1280]{1,0:T(8,128)(2,1)S(1)}, u32[]{:S(2)}, u32[]{:S(2)}) collective-permute-start(bf16[32,1280]{1,0:T(8,128)(2,1)S(1)} %pad_maximum_fusion.4), channel_id=1, source_target_pairs={{0,3},{1,2},{2,1},{3,0},{4,7},{5,6},{6,5},{7,4},{8,11},{9,10},{10,... | collective-permute-start | bytes 245768 | tf_op jit(solution)/shard_map/ppermute | solution.py:386
  22.7 10.3 %collective-permute-start.3 = (bf16[32,1280]{1,0:T(8,128)(2,1)S(1)}, bf16[32,1280]{1,0:T(8,128)(2,1)S(1)}, u32[]{:S(2)}, u32[]{:S(2)}) collective-permute-start(bf16[32,1280]{1,0:T(8,128)(2,1)S(1)} %pad_maximum_fusion.5), channel_id=1, source_target_pairs={{0,4},{1,5},{2,6},{3,7},{4,0},{5,1},{6,2},{7,3},{8,12},{9,13},{10,... | collective-permute-start | bytes 245768 | tf_op jit(solution)/shard_map/ppermute | solution.py:386
  23.2 9.8 %collective-permute-start.4 = (bf16[32,1280]{1,0:T(8,128)(2,1)S(1)}, bf16[32,1280]{1,0:T(8,128)(2,1)S(1)}, u32[]{:S(2)}, u32[]{:S(2)}) collective-permute-start(bf16[32,1280]{1,0:T(8,128)(2,1)S(1)} %pad_maximum_fusion.6), channel_id=1, source_target_pairs={{0,5},{1,4},{2,7},{3,6},{4,1},{5,0},{6,3},{7,2},{8,13},{9,12},{10,... | collective-permute-start | bytes 245768 | tf_op jit(solution)/shard_map/ppermute | solution.py:386
  27.4 6.5 %collective-permute-start.5 = (bf16[32,1280]{1,0:T(8,128)(2,1)S(1)}, bf16[32,1280]{1,0:T(8,128)(2,1)S(1)}, u32[]{:S(2)}, u32[]{:S(2)}) collective-permute-start(bf16[32,1280]{1,0:T(8,128)(2,1)S(1)} %pad_maximum_fusion.7), channel_id=1, source_target_pairs={{0,6},{1,7},{2,4},{3,5},{4,2},{5,3},{6,0},{7,1},{8,14},{9,15},{10,... | collective-permute-start | bytes 245768 | tf_op jit(solution)/shard_map/ppermute | solution.py:386
  31.3 6.6 %collective-permute-start.6 = (bf16[32,1280]{1,0:T(8,128)(2,1)S(1)}, bf16[32,1280]{1,0:T(8,128)(2,1)S(1)}, u32[]{:S(2)}, u32[]{:S(2)}) collective-permute-start(bf16[32,1280]{1,0:T(8,128)(2,1)S(1)} %pad_maximum_fusion.8), channel_id=1, source_target_pairs={{0,7},{1,6},{2,5},{3,4},{4,3},{5,2},{6,1},{7,0},{8,15},{9,14},{10,... | collective-permute-start | bytes 245768 | tf_op jit(solution)/shard_map/ppermute | solution.py:386
  33.0 63.1 %copy-start.2 = (s32[3]{0:T(128)}, s32[3]{0:T(128)S(1)}, u32[]{:S(2)}) copy-start(s32[3]{0:T(128)S(1)} %pad_add_fusion.info) | copy-start | bytes 40
  42.3 1.4 copy-start.4
  43.6 1.0 copy-start.5
  44.6 8.9 %collective-permute-start.9 = (bf16[8,2,16,128]{3,2,1,0:T(8,128)(2,1)S(1)}, bf16[8,2,16,128]{3,2,1,0:T(8,128)(2,1)S(1)}, u32[]{:S(2)}, u32[]{:S(2)}) collective-permute-start(bf16[8,2,16,128]{3,2,1,0:T(8,128)(2,1)S(1)} %get-tuple-element.40), channel_id=1, source_target_pairs={{0,24},{8,16},{16,8},{24,0},{32,56},{40,48},{48,40},{56,32},{64,88... | collective-permute-start | bytes 196616 | tf_op jit(solution)/shard_map/ppermute | solution.py:402
  51.0 5.6 %collective-permute-start.8 = (bf16[8,2,16,128]{3,2,1,0:T(8,128)(2,1)S(1)}, bf16[8,2,16,128]{3,2,1,0:T(8,128)(2,1)S(1)}, u32[]{:S(2)}, u32[]{:S(2)}) collective-permute-start(bf16[8,2,16,128]{3,2,1,0:T(8,128)(2,1)S(1)} %get-tuple-element.41), channel_id=1, source_target_pairs={{0,16},{8,24},{16,0},{24,8},{32,48},{40,56},{48,32},{56,40},{64,80... | collective-permute-start | bytes 196616 | tf_op jit(solution)/shard_map/ppermute | solution.py:402
  53.0 3.6 %collective-permute-start.7 = (bf16[8,2,16,128]{3,2,1,0:T(8,128)(2,1)S(1)}, bf16[8,2,16,128]{3,2,1,0:T(8,128)(2,1)S(1)}, u32[]{:S(2)}, u32[]{:S(2)}) collective-permute-start(bf16[8,2,16,128]{3,2,1,0:T(8,128)(2,1)S(1)} %get-tuple-element.42), channel_id=1, source_target_pairs={{0,8},{8,0},{16,24},{24,16},{32,40},{40,32},{48,56},{56,48},{64,72... | collective-permute-start | bytes 196616 | tf_op jit(solution)/shard_map/ppermute | solution.py:402
  92.5 92.5 %all-to-all-start.1 = ((bf16[8,4,2,16,128]{4,3,2,1,0:T(8,128)(2,1)}), bf16[8,4,2,16,128]{4,3,2,1,0:T(8,128)(2,1)S(1)}, u32[]{:S(2)}, u32[]{:S(2)}) async-start(bf16[8,4,2,16,128]{4,3,2,1,0:T(8,128)(2,1)} %pad_maximum_fusion), calls=%async_computation.1 | async-start | bytes 524288 | tf_op jit(solution)/shard_map/all_to_all | solution.py:408
  96.1 93.5 %copy-start = (bf16[256,16,128]{2,1,0:T(8,128)(2,1)S(1)}, bf16[256,16,128]{2,1,0:T(8,128)(2,1)}, u32[]{:S(2)}) copy-start(bf16[256,16,128]{2,1,0:T(8,128)(2,1)} %keys.1) | copy-start | bytes 3145732
  96.1 93.5 %copy-start.1 = (bf16[256,16,128]{2,1,0:T(8,128)(2,1)S(1)}, bf16[256,16,128]{2,1,0:T(8,128)(2,1)}, u32[]{:S(2)}) copy-start(bf16[256,16,128]{2,1,0:T(8,128)(2,1)} %values.1) | copy-start | bytes 3145732
  185.0 14.1 %all-to-all-start.2 = ((bf16[8,32,1024]{2,1,0:T(8,128)(2,1)}), bf16[8,32,1024]{2,1,0:T(8,128)(2,1)S(1)}, u32[]{:S(2)}, u32[]{:S(2)}) async-start(bf16[8,32,1024]{2,1,0:T(8,128)(2,1)} %bitcast.27), calls=%async_computation.2 | async-start | bytes 1048576 | tf_op jit(solution)/shard_map/all_to_all | solution.py:414
  (1 other events, 0.6 us)

commit v4 on v3

--- a/solution.py
+++ b/solution.py
@@ -1,3 +1,5 @@
+import functools
+
 import jax
 import jax.numpy as jnp
 from jax import lax
@@ -20,7 +22,7 @@
 TOK = 256
 NEWB = TOK // BLK
 LOAD = 2 * CAP
-PART = 8
+PART = 4
 WIDE = 57 * 1024 * 1024
 SCALE = HD ** (-0.5) * 1.4426950408889634
 neg_big = -1e30
@@ -142,7 +144,7 @@
 
 def gather_kernel(info, evict, *refs):
     pieces = refs[:TENSOR]
-    heads, start, sends, own_keys, own_values = refs[TENSOR:]
+    heads, own_keys, own_values, sends = refs[TENSOR:]
     t, count, me = info[0], info[1], info[2]
     lane = me & (LANES - 1)
     rows = TOK // TENSOR
@@ -150,7 +152,7 @@
         begin = pl.multiple_of((t ^ k) * rows, rows)
         at = pl.ds(begin, rows)
         for h in range(GROUP):
-            heads[pl.ds(pl.multiple_of(h * TOK + begin, rows), rows), :HD] = pieces[k][
+            heads[pl.ds(pl.multiple_of(h * TOK + begin, rows), rows), :] = pieces[k][
                 :, h * HD : (h + 1) * HD
             ]
         own_keys[at, :] = pieces[k][:, GROUP * HD : (GROUP + 1) * HD]
@@ -162,32 +164,19 @@
         for part, own in enumerate((own_keys, own_values)):
             block = own[j * BLK : (j + 1) * BLK, :]
             sends[(owner & (LANES - 1)) ^ lane, owner // LANES, part] = jnp.where(live, block.astype(f32), 0.0).astype(bf16)
-    both = with_ones(own_values[...])
-    row = lax.broadcasted_iota(i32, (TOK, TOK), 0)
-    column = lax.broadcasted_iota(i32, (TOK, TOK), 1)
-
-    @pl.loop(0, GROUP)
-    def _(h):
-        at = pl.ds(pl.multiple_of(h * TOK, TOK), TOK)
-        scores = lax.dot_general(heads[at, :HD], own_keys[...], NT, preferred_element_type=f32)
-        scores = jnp.where(column <= row, scores * SCALE, neg_big)
-        top = jnp.max(scores, axis=1, keepdims=True).astype(bf16)
-        heads[at, HD:] = jnp.broadcast_to(top, (TOK, HD))
-        weights = jnp.exp2(scores - top.astype(f32)).astype(bf16)
-        start[at, :] = jnp.dot(weights, both, preferred_element_type=f32)
 
 
 def gather(info, evict_slots, pieces):
     return pl.pallas_call(
         gather_kernel,
         out_shape=[
-            jax.ShapeDtypeStruct((GROUP * TOK, 2 * HD), bf16),
-            jax.ShapeDtypeStruct((GROUP * TOK, 2 * HD), f32),
+            jax.ShapeDtypeStruct((GROUP * TOK, HD), bf16),
+            jax.ShapeDtypeStruct((TOK, HD), bf16),
+            jax.ShapeDtypeStruct((TOK, HD), bf16),
             jax.ShapeDtypeStruct((LANES, LEVELS, 2, BLK, HD), bf16),
         ],
         in_specs=[SMEM, SMEM] + [VMEM] * TENSOR,
-        out_specs=[VMEM] * 3,
-        scratch_shapes=[pltpu.VMEM((TOK, HD), bf16), pltpu.VMEM((TOK, HD), bf16)],
+        out_specs=[VMEM] * 4,
         compiler_params=pltpu.CompilerParams(vmem_limit_bytes=16 * 1024 * 1024),
         cost_estimate=cost(10**9, 4 * 10**6),
         name="gather_rows",
@@ -223,54 +212,57 @@
 KEYS = PBLK * BLK
 ROWS = 1024
 TILE = 256
-SMALL = 256
 SPLIT = 8
 
 
-def attend_kernel(info, where_from, heads_h, start_h, got_h, out_h, *scratch):
-    got, keys, values, heads, start, out, sems, got_sems, out_sems = scratch
+def attend_kernel(info, where_from, heads_h, own_keys_h, own_values_h, got_h, out_h, *scratch):
+    got, keys, values, heads, own_keys, own_values, shift, start, out, sems, got_sems, out_sem = (
+        scratch
+    )
     blocks = GROUP * TOK // ROWS
     part = got.shape[0] // SPLIT
     coming = []
     for i in range(SPLIT):
         at = pl.ds(i * part, part)
         coming.append(pltpu.make_async_copy(got_h.at[at], got.at[at], got_sems.at[i]))
-    head_copies, start_copies = [], []
-    for i in range(blocks):
-        rows = pl.ds(i * ROWS, ROWS)
-        head_copies.append(
-            pltpu.make_async_copy(heads_h.at[rows], heads.at[rows], sems.at[i, 0])
+    first = [
+        pltpu.make_async_copy(source, target, sems.at[i])
+        for i, (source, target) in enumerate(
+            ((own_keys_h, own_keys), (own_values_h, own_values), (heads_h, heads))
         )
-        start_copies.append(
-            pltpu.make_async_copy(start_h.at[rows], start.at[rows], sems.at[i, 1])
-        )
-    for copy in coming + head_copies[:1]:
+    ]
+    for copy in first + coming:
         copy.start()
+    for copy in first:
+        copy.wait()
+
+    both = with_ones(own_values[...])
+    row = lax.broadcasted_iota(i32, (TOK, TOK), 0)
+    column = lax.broadcasted_iota(i32, (TOK, TOK), 1)
+    for h in range(GROUP):
+        at = slice(h * TOK, (h + 1) * TOK)
+        scores = lax.dot_general(heads[at, :], own_keys[...], NT, preferred_element_type=f32)
+        scores = jnp.where(column <= row, scores * SCALE, neg_big)
+        top = jnp.max(scores, axis=1, keepdims=True)
+        shift[at, :] = jnp.broadcast_to(top, (TOK, HD))
+        weights = jnp.exp2(scores - top).astype(bf16)
+        start[at, :] = jnp.dot(weights, both, preferred_element_type=f32)
+
     for copy in coming:
         copy.wait()
-    for copy in head_copies[1:] + start_copies:
-        copy.start()
     for b in range(PBLK):
         index = where_from[b]
         keys[b * BLK : (b + 1) * BLK, :] = got[index]
         values[b * BLK : (b + 1) * BLK, :] = got[index + CAP]
     live = lax.broadcasted_iota(i32, (TOK, HD), 0) < info[1]
-    leaving = [
-        pltpu.make_async_copy(
-            out.at[:, pl.ds(h * HD, HD)], out_h.at[:, pl.ds(h * HD, HD)], out_sems.at[h]
-        )
-        for h in range(GROUP)
-    ]
-
-    def finish(h, summed):
-        result = summed[:, :HD] / summed[:, HD:]
-        out[:, h * HD : (h + 1) * HD] = jnp.where(live, result, 0.0).astype(bf16)
+    largest = []
+    def result_of(summed):
+        return jnp.where(live, summed[:, :HD] / summed[:, HD:], 0.0).astype(bf16)
 
     for i in range(blocks):
-        head_copies[i].wait()
-        query = heads[i * ROWS : (i + 1) * ROWS, :HD]
-        top = heads[i * ROWS : (i + 1) * ROWS, HD:].astype(f32)
-        summed = None
+        query = heads[i * ROWS : (i + 1) * ROWS, :]
+        top = shift[i * ROWS : (i + 1) * ROWS, :]
+        summed = start[i * ROWS : (i + 1) * ROWS, :]
         for j in range(KEYS // TILE):
             tile = slice(j * TILE, (j + 1) * TILE)
             part = lax.dot_general(query, keys[tile, :], NT, preferred_element_type=f32)
@@ -281,71 +273,67 @@
                 ],
                 axis=1,
             ).astype(bf16)
-            more = jnp.dot(weights, with_ones(values[tile, :]), preferred_element_type=f32)
-            summed = more if summed is None else summed + more
-        start_copies[i].wait()
-        summed = summed + start[i * ROWS : (i + 1) * ROWS, :]
+            summed = summed + jnp.dot(
+                weights, with_ones(values[tile, :]), preferred_element_type=f32
+            )
         for h in range(ROWS // TOK):
-            finish(i * (ROWS // TOK) + h, summed[h * TOK : (h + 1) * TOK, :])
-        largest = jnp.max(summed[:, HD:])
-
-        @pl.when(jnp.logical_not(largest < 1e30))
-        def _():
-            for h in range(ROWS // TOK):
-                at = slice(i * ROWS + h * TOK, i * ROWS + (h + 1) * TOK)
-
-                def one(j, state):
-                    best, summed = state
-                    tile = pl.ds(pl.multiple_of(j * SMALL, SMALL), SMALL)
-                    part = (
-                        lax.dot_general(
-                            heads[at, :HD], keys[tile, :], NT, preferred_element_type=f32
-                        )
-                        * SCALE
-                    )
-                    above = jnp.maximum(best, jnp.max(part, axis=1, keepdims=True))
-                    weights = jnp.exp2(part - above).astype(bf16)
-                    summed = summed * jnp.exp2(best - above) + jnp.dot(
-                        weights, with_ones(values[tile, :]), preferred_element_type=f32
-                    )
-                    return above, summed
-
-                best, summed = lax.fori_loop(
-                    0,
-                    KEYS // SMALL,
-                    one,
-                    (heads[at, HD : HD + 1].astype(f32), start[at, :]),
+            head = i * (ROWS // TOK) + h
+            out[:, head * HD : (head + 1) * HD] = result_of(summed[h * TOK : (h + 1) * TOK, :])
+        largest.append(jnp.max(summed[:, HD:]))
+
+    @pl.when(jnp.logical_not(functools.reduce(jnp.maximum, largest) < 1e30))
+    def _():
+        @pl.loop(0, GROUP)
+        def _(h):
+            at = pl.ds(pl.multiple_of(h * TOK, TOK), TOK)
+
+            def one(j, state):
+                best, summed = state
+                tile = pl.ds(pl.multiple_of(j * TILE, TILE), TILE)
+                part = (
+                    lax.dot_general(heads[at, :], keys[tile, :], NT, preferred_element_type=f32)
+                    * SCALE
                 )
-                finish(i * (ROWS // TOK) + h, summed)
-
-        for h in range(i * (ROWS // TOK), (i + 1) * (ROWS // TOK)):
-            leaving[h].start()
-    for copy in leaving:
-        copy.wait()
-
-
-def attend(info, where_from, heads, start, got):
+                above = jnp.maximum(best, jnp.max(part, axis=1, keepdims=True))
+                weights = jnp.exp2(part - above).astype(bf16)
+                summed = summed * jnp.exp2(best - above) + jnp.dot(
+                    weights, with_ones(values[tile, :]), preferred_element_type=f32
+                )
+                return above, summed
+
+            best, summed = lax.fori_loop(0, KEYS // TILE, one, (shift[at, :1], start[at, :]))
+            out[:, pl.ds(pl.multiple_of(h * HD, HD), HD)] = result_of(summed)
+
+    leaving = pltpu.make_async_copy(out, out_h, out_sem)
+    leaving.start()
+    leaving.wait()
+
+
+def attend(info, where_from, heads, own_keys, own_values, got):
     blocks = got.shape[0] * got.shape[1]
     return pl.pallas_call(
         attend_kernel,
         out_shape=jax.ShapeDtypeStruct((TOK, GROUP * HD), bf16),
-        in_specs=[SMEM, SMEM, HBM, HBM, HBM],
+        in_specs=[SMEM, SMEM] + [HBM] * 4,
         out_specs=HBM,
         scratch_shapes=[
             pltpu.VMEM((blocks, BLK, HD), bf16),
             pltpu.VMEM((KEYS, HD), bf16),
             pltpu.VMEM((KEYS, HD), bf16),
             pltpu.VMEM(heads.shape, bf16),
-            pltpu.VMEM(start.shape, f32),
+            pltpu.VMEM((TOK, HD), bf16),
+            pltpu.VMEM((TOK, HD), bf16),
+            pltpu.VMEM(heads.shape, f32),
+            pltpu.VMEM((GROUP * TOK, 2 * HD), f32),
             pltpu.VMEM((TOK, GROUP * HD), bf16),
-            pltpu.SemaphoreType.DMA((GROUP * TOK // ROWS, 2)),
+            pltpu.SemaphoreType.DMA((3,)),
             pltpu.SemaphoreType.DMA((SPLIT,)),
-            pltpu.SemaphoreType.DMA((GROUP,)),
+            pltpu.SemaphoreType.DMA,
         ],
         compiler_params=pltpu.CompilerParams(vmem_limit_bytes=WIDE),
         cost_estimate=cost(9 * 10**9, 6 * 10**6, 9 * 10**6),
         name="attend",
-    )(info, where_from, heads, start, got.reshape(blocks, BLK, HD))
+    )(info, where_from, heads, own_keys, own_values, got.reshape(blocks, BLK, HD))
 
 
 def local(
@@ -397,7 +385,7 @@
 
     target = jnp.max(jnp.where(evict_slots // SLOTS == me, evict_slots % SLOTS, -1), axis=1)
 
-    heads, start, sends = gather(info, evict_slots, pieces)
+    heads, own_keys, own_values, sends = gather(info, evict_slots, pieces)
     turned = [sends[0]] + [
         lax.ppermute(sends[m], "pool", [(s, s ^ m) for s in range(POOL)])
         for m in range(1, LANES)
@@ -408,7 +396,7 @@
     arrived = lax.all_to_all(
         sends, "pool", split_axis=0, concat_axis=0, tiled=True, axis_index_groups=columns
     )
-    result = attend(info, where_from, heads, start, got)
+    result = attend(info, where_from, heads, own_keys, own_values, got)
     result, arrived = lax.optimization_barrier((result, arrived))
     result = result.reshape(TENSOR, share, GROUP * HD)
     attended = lax.all_to_all(result, "tensor", split_axis=0, concat_axis=0, tiled=True)

time: 200 us -> 200 us (level)
  waiting for transfers between devices: 49.8 us -> 53.5 us
  Pallas kernels: 100 us -> 96.5 us
    all_to_all x1, waiting for transfers between devices: 35.2 us -> 38.8 us  [local(): got = lax.all_to_all(send, 'pool', split_axis=0, concat_axis=0, tiled=True)]
    pallas_call x1, Pallas kernels: 4.41 us -> 1.04 us  [gather(): pl.pallas_call(gather_kernel, out_shape=[jax.ShapeDtypeStruct((GROUP * TO...]
  transfers between devices with their start and end apart: 13 -> 13, of which waited for: 5 -> 6; matrix products, arithmetic and copies ran while one was open for 3% -> 3% of each run, Pallas kernels for 48% -> 46%
where the time goes in v4:
time: 200 us
  Pallas kernels  96.5 us (48%)
  waiting for transfers between devices  53.5 us (27%)
  starting transfers between devices  39.6 us (20%)
  local copies, waits for them, and re-layouts  6.01 us (3%)
  other arithmetic  3.06 us (2%)
    pallas_call x1, Pallas kernels, attend(): pl.pallas_call(attend_kernel, out_shape=jax.ShapeDtypeStruct((TOK, GROUP...  88.7 us
    all_to_all x1, waiting for transfers between devices, local(): got = lax.all_to_all(send, 'pool', split_axis=0, concat_axis=0, tiled=True)  38.8 us
    all_to_all x1, starting transfers between devices, local(): got = lax.all_to_all(send, 'pool', split_axis=0, concat_axis=0, tiled=True)  12.9 us
    ppermute x7, starting transfers between devices, local(): piece = lax.ppermute(piece, 'tensor', [(s, s ^ k) for s in range(TENSOR)])  10.3 us
    ppermute x3, starting transfers between devices, local(): lax.ppermute(sends[m], 'pool', [(s, s ^ m) for s in range(POOL)])  8.23 us
    all_to_all x1, waiting for transfers between devices, local(): lax.all_to_all(result, 'tensor', split_axis=0, concat_axis=0, tiled=True)  6.68 us
    ppermute x7, waiting for transfers between devices, local(): piece = lax.ppermute(piece, 'tensor', [(s, s ^ k) for s in range(TENSOR)])  4.88 us
    all_to_all x1, starting transfers between devices, local(): lax.all_to_all(result, 'tensor', split_axis=0, concat_axis=0, tiled=True)  4.55 us
  transfers between devices with their start and end apart: 13, of which 6 were waited for; matrix products, arithmetic and copies ran while one was open for 3% of the time, Pallas kernels for 46%

profile of v4, /device:TPU:1, one launch (start us, length us, event | category | flops | bytes accessed | tf_op | source)
XLA Modules:
  0.0 199.7 jit_solution(11440612456448716060)
XLA Ops:
  0.6 4.5 %pack_blocks.1 = bf16[32,24,16,128]{3,2,1,0:T(8,128)(2,1)} custom-call(s32[1]{0:T(128)} %bitcast.1.me, s32[32,256]{1,0:T(8,128)} %prefix_h.1, s32[64,128]{1,0:T(8,128)} %bitcast.25, s32[64,128]{1,0:T(8,128)} %bitcast.32, bf16[256,16,128]{2,1,0:T(8,128)(2,1)} %keys.1, bf16[256,16,128]{2,1,0:T(8,128)(2,1)} %values.1), custom_call_target="tpu_custom_call" | custom-call | flops 1000000000 | bytes 5000000 | tf_op jit(solution)/shard_map/pack_blocks/pallas_call | solution.py:114
  5.2 12.9 %all-to-all-start = ((bf16[32,24,16,128]{3,2,1,0:T(8,128)(2,1)}), bf16[32,24,16,128]{3,2,1,0:T(8,128)(2,1)}, u32[]{:S(2)}, u32[]{:S(2)}) async-start(bf16[32,24,16,128]{3,2,1,0:T(8,128)(2,1)} %pack_blocks.1), calls=%async_computation | async-start | bytes 6291456 | tf_op jit(solution)/shard_map/all_to_all | solution.py:360
  18.5 1.3 collective-permute-start
  19.8 2.5 %collective-permute-start.1 = (bf16[32,1280]{1,0:T(8,128)(2,1)S(1)}, bf16[32,1280]{1,0:T(8,128)(2,1)S(1)}, u32[]{:S(2)}, u32[]{:S(2)}) collective-permute-start(bf16[32,1280]{1,0:T(8,128)(2,1)S(1)} %pad_maximum_fusion.3), channel_id=1, source_target_pairs={{0,2},{1,3},{2,0},{3,1},{4,6},{5,7},{6,4},{7,5},{8,10},{9,11},{10,... | collective-permute-start | bytes 245768 | tf_op jit(solution)/shard_map/ppermute | solution.py:374
  23.1 0.9 collective-permute-start.4
  25.3 1.7 gather_fusion
  27.4 3.9 %collective-permute-start.5 = (bf16[32,1280]{1,0:T(8,128)(2,1)S(1)}, bf16[32,1280]{1,0:T(8,128)(2,1)S(1)}, u32[]{:S(2)}, u32[]{:S(2)}) collective-permute-start(bf16[32,1280]{1,0:T(8,128)(2,1)S(1)} %pad_maximum_fusion.7), channel_id=1, source_target_pairs={{0,6},{1,7},{2,4},{3,5},{4,2},{5,3},{6,0},{7,1},{8,14},{9,15},{10,... | collective-permute-start | bytes 245768 | tf_op jit(solution)/shard_map/ppermute | solution.py:374
  31.2 1.0 collective-permute-start.6
  32.2 0.7 pad_add_fusion.info
  32.9 0.9 collective-permute-done.5.refs_6_
  33.8 4.0 %collective-permute-done.6.refs_7_ = bf16[32,1280]{1,0:T(8,128)(2,1)S(1)} collective-permute-done((bf16[32,1280]{1,0:T(8,128)(2,1)S(1)}, bf16[32,1280]{1,0:T(8,128)(2,1)S(1)}, u32[]{:S(2)}, u32[]{:S(2)}) %collective-permute-start.6) | collective-permute-done | bytes 81952 | tf_op jit(solution)/shard_map/ppermute | solution.py:374
  37.8 1.0 gather_rows.1
  40.1 0.8 copy-done.4
  40.9 6.3 %collective-permute-start.9 = (bf16[8,2,16,128]{3,2,1,0:T(8,128)(2,1)S(1)}, bf16[8,2,16,128]{3,2,1,0:T(8,128)(2,1)S(1)}, u32[]{:S(2)}, u32[]{:S(2)}) collective-permute-start(bf16[8,2,16,128]{3,2,1,0:T(8,128)(2,1)S(1)} %get-tuple-element.42), channel_id=1, source_target_pairs={{0,24},{8,16},{16,8},{24,0},{32,56},{40,48},{48,40},{56,32},{64,88... | collective-permute-start | bytes 196616 | tf_op jit(solution)/shard_map/ppermute | solution.py:390
  47.2 2.0 collective-permute-start.8
  50.1 2.8 %collective-permute-done.8 = bf16[8,2,16,128]{3,2,1,0:T(8,128)(2,1)S(1)} collective-permute-done((bf16[8,2,16,128]{3,2,1,0:T(8,128)(2,1)S(1)}, bf16[8,2,16,128]{3,2,1,0:T(8,128)(2,1)S(1)}, u32[]{:S(2)}, u32[]{:S(2)}) %collective-permute-start.8) | collective-permute-done | bytes 65568 | tf_op jit(solution)/shard_map/ppermute | solution.py:390
  52.9 0.7 pad_maximum_fusion
  53.6 38.8 %all-to-all-done = bf16[32,24,16,128]{3,2,1,0:T(8,128)(2,1)} async-done(((bf16[32,24,16,128]{3,2,1,0:T(8,128)(2,1)}), bf16[32,24,16,128]{3,2,1,0:T(8,128)(2,1)}, u32[]{:S(2)}, u32[]{:S(2)}) %all-to-all-start) | async-done | bytes 3145760 | tf_op jit(solution)/shard_map/all_to_all | solution.py:360
  92.4 3.6 %all-to-all-start.1 = ((bf16[8,4,2,16,128]{4,3,2,1,0:T(8,128)(2,1)}), bf16[8,4,2,16,128]{4,3,2,1,0:T(8,128)(2,1)S(1)}, u32[]{:S(2)}, u32[]{:S(2)}) async-start(bf16[8,4,2,16,128]{4,3,2,1,0:T(8,128)(2,1)} %pad_maximum_fusion), calls=%async_computation.1 | async-start | bytes 524288 | tf_op jit(solution)/shard_map/all_to_all | solution.py:396
  96.0 88.7 %attend.1 = bf16[256,1024]{1,0:T(8,128)(2,1)} custom-call(s32[3]{0:T(128)} %copy-done.2, s32[256]{0:T(256)} %add_subtract_fusion.where_from, bf16[2048,128]{1,0:T(8,128)(2,1)} %copy-done.4, bf16[256,128]{1,0:T(8,128)(2,1)} %copy-done.5, bf16[256,128]{1,0:T(8,128)(2,1)} %copy-done.6, bf16[768,16,128]{2,1,0:T(8,128)(2,1)} %bitcast.13.got_h), custom_call_target="tpu_custom_call" | custom-call | flops 8999999488 | bytes 6000000 | tf_op jit(solution)/shard_map/attend/pallas_call | solution.py:314
  184.7 4.5 %all-to-all-start.2 = ((bf16[8,32,1024]{2,1,0:T(8,128)(2,1)}), bf16[8,32,1024]{2,1,0:T(8,128)(2,1)S(1)}, u32[]{:S(2)}, u32[]{:S(2)}) async-start(bf16[8,32,1024]{2,1,0:T(8,128)(2,1)} %bitcast.27), calls=%async_computation.2 | async-start | bytes 1048576 | tf_op jit(solution)/shard_map/all_to_all | solution.py:402
  189.9 2.3 %write_blocks.1 = (bf16[256,16,128]{2,1,0:T(8,128)(2,1)}, bf16[256,16,128]{2,1,0:T(8,128)(2,1)}) custom-call(s32[3]{0:T(128)S(1)} %copy-done.3, s32[32]{0:T(128)S(1)} %fusion.2.target, bf16[256,16,128]{2,1,0:T(8,128)(2,1)S(1)} %copy-done, bf16[256,16,128]{2,1,0:T(8,128)(2,1)S(1)} %copy-done.1, bf16[8,4,2,16,128]{4,3,2,1,0:T(8,128)(2,1)S(1)} %all-to-all-done.1.arrived), custom_call_target="tpu_custom_call" | custom-call | flops 1000000 | bytes 4000000 | tf_op jit(solution)/shard_map/write_blocks/pallas_call | solution.py:201
  192.2 6.7 %all-to-all-done.2 = bf16[8,32,1024]{2,1,0:T(8,128)(2,1)S(1)} async-done(((bf16[8,32,1024]{2,1,0:T(8,128)(2,1)}), bf16[8,32,1024]{2,1,0:T(8,128)(2,1)S(1)}, u32[]{:S(2)}, u32[]{:S(2)}) %all-to-all-start.2) | async-done | bytes 524320 | tf_op jit(solution)/shard_map/all_to_all | solution.py:402
  198.9 0.8 copy.19
  (55 shorter events, 5.4 us)
Async XLA Ops:
  5.2 13.1 %copy-start.9 = (bf16[32,1024]{1,0:T(8,128)(2,1)S(1)}, bf16[32,1024]{1,0:T(8,128)(2,1)}, u32[]{:S(2)}) copy-start(bf16[32,1024]{1,0:T(8,128)(2,1)} %param.12) | copy-start | bytes 196612
  5.2 13.1 %copy-start.10 = (bf16[32,1024]{1,0:T(8,128)(2,1)S(1)}, bf16[32,1024]{1,0:T(8,128)(2,1)}, u32[]{:S(2)}) copy-start(bf16[32,1024]{1,0:T(8,128)(2,1)} %param.11) | copy-start | bytes 196612
  5.2 13.2 %copy-start.8 = (bf16[32,8192]{1,0:T(8,128)(2,1)S(1)}, bf16[32,8192]{1,0:T(8,128)(2,1)}, u32[]{:S(2)}) copy-start(bf16[32,8192]{1,0:T(8,128)(2,1)} %param.10) | copy-start | bytes 1572868
  5.2 18.7 %copy-start.12 = (s32[32]{0:T(128)S(1)}, s32[32]{0:T(128)}, u32[]{:S(2)}) copy-start(s32[32]{0:T(128)} %param.19) | copy-start | bytes 388
  5.2 20.0 %copy-start.7 = (s32[8192]{0:T(1024)S(1)}, s32[8192]{0:T(1024)}, u32[]{:S(2)}) copy-start(s32[8192]{0:T(1024)} %param.16) | copy-start | bytes 98308
  5.2 87.2 %all-to-all-start = ((bf16[32,24,16,128]{3,2,1,0:T(8,128)(2,1)}), bf16[32,24,16,128]{3,2,1,0:T(8,128)(2,1)}, u32[]{:S(2)}, u32[]{:S(2)}) async-start(bf16[32,24,16,128]{3,2,1,0:T(8,128)(2,1)} %pack_blocks.1), calls=%async_computation | async-start | bytes 6291456 | tf_op jit(solution)/shard_map/all_to_all | solution.py:360
  18.2 8.8 %copy-start.11 = (s32[32,16]{0,1:T(8,128)S(1)}, s32[32,16]{0,1:T(8,128)}, u32[]{:S(2)}) copy-start(s32[32,16]{0,1:T(8,128)} %param.18) | copy-start | bytes 6148
  18.5 8.9 %collective-permute-start = (bf16[32,1280]{1,0:T(8,128)(2,1)S(1)}, bf16[32,1280]{1,0:T(8,128)(2,1)S(1)}, u32[]{:S(2)}, u32[]{:S(2)}) collective-permute-start(bf16[32,1280]{1,0:T(8,128)(2,1)S(1)} %pad_maximum_fusion.2), channel_id=1, source_target_pairs={{0,1},{1,0},{2,3},{3,2},{4,5},{5,4},{6,7},{7,6},{8,9},{9,8},{10,11... | collective-permute-start | bytes 245768 | tf_op jit(solution)/shard_map/ppermute | solution.py:374
  19.8 11.4 %collective-permute-start.1 = (bf16[32,1280]{1,0:T(8,128)(2,1)S(1)}, bf16[32,1280]{1,0:T(8,128)(2,1)S(1)}, u32[]{:S(2)}, u32[]{:S(2)}) collective-permute-start(bf16[32,1280]{1,0:T(8,128)(2,1)S(1)} %pad_maximum_fusion.3), channel_id=1, source_target_pairs={{0,2},{1,3},{2,0},{3,1},{4,6},{5,7},{6,4},{7,5},{8,10},{9,11},{10,... | collective-permute-start | bytes 245768 | tf_op jit(solution)/shard_map/ppermute | solution.py:374
  22.3 10.6 %collective-permute-start.2 = (bf16[32,1280]{1,0:T(8,128)(2,1)S(1)}, bf16[32,1280]{1,0:T(8,128)(2,1)S(1)}, u32[]{:S(2)}, u32[]{:S(2)}) collective-permute-start(bf16[32,1280]{1,0:T(8,128)(2,1)S(1)} %pad_maximum_fusion.4), channel_id=1, source_target_pairs={{0,3},{1,2},{2,1},{3,0},{4,7},{5,6},{6,5},{7,4},{8,11},{9,10},{10,... | collective-permute-start | bytes 245768 | tf_op jit(solution)/shard_map/ppermute | solution.py:374
  22.6 10.3 %collective-permute-start.3 = (bf16[32,1280]{1,0:T(8,128)(2,1)S(1)}, bf16[32,1280]{1,0:T(8,128)(2,1)S(1)}, u32[]{:S(2)}, u32[]{:S(2)}) collective-permute-start(bf16[32,1280]{1,0:T(8,128)(2,1)S(1)} %pad_maximum_fusion.5), channel_id=1, source_target_pairs={{0,4},{1,5},{2,6},{3,7},{4,0},{5,1},{6,2},{7,3},{8,12},{9,13},{10,... | collective-permute-start | bytes 245768 | tf_op jit(solution)/shard_map/ppermute | solution.py:374
  23.1 9.8 %collective-permute-start.4 = (bf16[32,1280]{1,0:T(8,128)(2,1)S(1)}, bf16[32,1280]{1,0:T(8,128)(2,1)S(1)}, u32[]{:S(2)}, u32[]{:S(2)}) collective-permute-start(bf16[32,1280]{1,0:T(8,128)(2,1)S(1)} %pad_maximum_fusion.6), channel_id=1, source_target_pairs={{0,5},{1,4},{2,7},{3,6},{4,1},{5,0},{6,3},{7,2},{8,13},{9,12},{10,... | collective-permute-start | bytes 245768 | tf_op jit(solution)/shard_map/ppermute | solution.py:374
  27.4 6.5 %collective-permute-start.5 = (bf16[32,1280]{1,0:T(8,128)(2,1)S(1)}, bf16[32,1280]{1,0:T(8,128)(2,1)S(1)}, u32[]{:S(2)}, u32[]{:S(2)}) collective-permute-start(bf16[32,1280]{1,0:T(8,128)(2,1)S(1)} %pad_maximum_fusion.7), channel_id=1, source_target_pairs={{0,6},{1,7},{2,4},{3,5},{4,2},{5,3},{6,0},{7,1},{8,14},{9,15},{10,... | collective-permute-start | bytes 245768 | tf_op jit(solution)/shard_map/ppermute | solution.py:374
  31.2 6.6 %collective-permute-start.6 = (bf16[32,1280]{1,0:T(8,128)(2,1)S(1)}, bf16[32,1280]{1,0:T(8,128)(2,1)S(1)}, u32[]{:S(2)}, u32[]{:S(2)}) collective-permute-start(bf16[32,1280]{1,0:T(8,128)(2,1)S(1)} %pad_maximum_fusion.8), channel_id=1, source_target_pairs={{0,7},{1,6},{2,5},{3,4},{4,3},{5,2},{6,1},{7,0},{8,15},{9,14},{10,... | collective-permute-start | bytes 245768 | tf_op jit(solution)/shard_map/ppermute | solution.py:374
  32.9 63.1 %copy-start.2 = (s32[3]{0:T(128)}, s32[3]{0:T(128)S(1)}, u32[]{:S(2)}) copy-start(s32[3]{0:T(128)S(1)} %pad_add_fusion.info) | copy-start | bytes 40
  38.9 0.6 copy-start.5
  40.1 0.8 copy-start.4
  40.9 9.2 %collective-permute-start.9 = (bf16[8,2,16,128]{3,2,1,0:T(8,128)(2,1)S(1)}, bf16[8,2,16,128]{3,2,1,0:T(8,128)(2,1)S(1)}, u32[]{:S(2)}, u32[]{:S(2)}) collective-permute-start(bf16[8,2,16,128]{3,2,1,0:T(8,128)(2,1)S(1)} %get-tuple-element.42), channel_id=1, source_target_pairs={{0,24},{8,16},{16,8},{24,0},{32,56},{40,48},{48,40},{56,32},{64,88... | collective-permute-start | bytes 196616 | tf_op jit(solution)/shard_map/ppermute | solution.py:390
  47.2 5.7 %collective-permute-start.8 = (bf16[8,2,16,128]{3,2,1,0:T(8,128)(2,1)S(1)}, bf16[8,2,16,128]{3,2,1,0:T(8,128)(2,1)S(1)}, u32[]{:S(2)}, u32[]{:S(2)}) collective-permute-start(bf16[8,2,16,128]{3,2,1,0:T(8,128)(2,1)S(1)} %get-tuple-element.43), channel_id=1, source_target_pairs={{0,16},{8,24},{16,0},{24,8},{32,48},{40,56},{48,32},{56,40},{64,80... | collective-permute-start | bytes 196616 | tf_op jit(solution)/shard_map/ppermute | solution.py:390
  49.1 3.8 %collective-permute-start.7 = (bf16[8,2,16,128]{3,2,1,0:T(8,128)(2,1)S(1)}, bf16[8,2,16,128]{3,2,1,0:T(8,128)(2,1)S(1)}, u32[]{:S(2)}, u32[]{:S(2)}) collective-permute-start(bf16[8,2,16,128]{3,2,1,0:T(8,128)(2,1)S(1)} %get-tuple-element.44), channel_id=1, source_target_pairs={{0,8},{8,0},{16,24},{24,16},{32,40},{40,32},{48,56},{56,48},{64,72... | collective-permute-start | bytes 196616 | tf_op jit(solution)/shard_map/ppermute | solution.py:390
  92.4 92.3 %all-to-all-start.1 = ((bf16[8,4,2,16,128]{4,3,2,1,0:T(8,128)(2,1)}), bf16[8,4,2,16,128]{4,3,2,1,0:T(8,128)(2,1)S(1)}, u32[]{:S(2)}, u32[]{:S(2)}) async-start(bf16[8,4,2,16,128]{4,3,2,1,0:T(8,128)(2,1)} %pad_maximum_fusion), calls=%async_computation.1 | async-start | bytes 524288 | tf_op jit(solution)/shard_map/all_to_all | solution.py:396
  96.0 93.3 %copy-start = (bf16[256,16,128]{2,1,0:T(8,128)(2,1)S(1)}, bf16[256,16,128]{2,1,0:T(8,128)(2,1)}, u32[]{:S(2)}) copy-start(bf16[256,16,128]{2,1,0:T(8,128)(2,1)} %keys.1) | copy-start | bytes 3145732
  96.0 93.3 %copy-start.1 = (bf16[256,16,128]{2,1,0:T(8,128)(2,1)S(1)}, bf16[256,16,128]{2,1,0:T(8,128)(2,1)}, u32[]{:S(2)}) copy-start(bf16[256,16,128]{2,1,0:T(8,128)(2,1)} %values.1) | copy-start | bytes 3145732
  184.7 14.1 %all-to-all-start.2 = ((bf16[8,32,1024]{2,1,0:T(8,128)(2,1)}), bf16[8,32,1024]{2,1,0:T(8,128)(2,1)S(1)}, u32[]{:S(2)}, u32[]{:S(2)}) async-start(bf16[8,32,1024]{2,1,0:T(8,128)(2,1)} %bitcast.27), calls=%async_computation.2 | async-start | bytes 1048576 | tf_op jit(solution)/shard_map/all_to_all | solution.py:402
  (2 other events, 1.2 us)
